TPU v7x, 32 devices: a whole 2x2x4 slice. The times are simulated.
32 devices in a mesh: parts: 2 (over y), tensor: 4 (over z), dp: 4 (over x, core).
Axes of the slice: x: 2, y: 2, z: 4, core: 2. Of those that a mesh axis runs over, the one named last changes fastest.
Arguments:
- inputs: bfloat16 [4096, 8192], P(('parts', 'dp'), 'tensor'), parts along dimension 0, may hold values from -6 to 6
- out_grad: bfloat16 [4096, 4, 2048], P(('parts', 'dp'), None, 'tensor'), parts along dimension 0, may hold values from -6 to 6
- gate_pre: bfloat16 [4096, 28672], P(('parts', 'dp'), 'tensor'), parts along dimension 0, may hold values from -8 to 8
- down_weight: bfloat16 [28672, 8192], P('tensor', 'dp'), may hold values from -0.03125 to 0.03125
- proj_in: bfloat16 [8192, 64], P('tensor'), may hold values from -0.0625 to 0.0625
- proj_out: bfloat16 [28672, 64], P('tensor'), may hold values from -0.09375 to 0.09375
- queries: bfloat16 [256, 4096], P('tensor', 'dp'), may hold values from -0.1875 to 0.1875
Outputs:
- scores: float32 [256, 4096], P('tensor', ('parts', 'dp')), parts along dimension 1
There are 2 independent parts, one for each index of `parts`. A program takes and returns all parts, laid end to end along the dimension named above; an argument that names none is the same for every part. Nothing has to cross between parts.
All inputs are finite; a program needn't handle non-finite values.
Results may differ from a plain program's by a relative error of at most 0.0041.
Values may be sent and summed in bfloat16 or wider, within the bound.
No kernel may reach another device: no remote copies, remote signals or barrier semaphores. Data moves between devices by JAX's collectives and lax.ppermute only.
A program may use at most 320 MiB of HBM per device.

v0:
```python
import functools

import jax
import jax.numpy as jnp
from jax import lax
from jax.experimental import pallas as pl
from jax.experimental.pallas import tpu as pltpu
from jax.sharding import PartitionSpec as P

TILE = 1024
SMALL = 512
RING = 4
VMEM = 60 * 1024 * 1024
ANY = pl.BlockSpec(memory_space=pl.ANY)


def swap(value, axis, size, mask):
    return lax.ppermute(value, axis, [(i, i ^ mask) for i in range(size)])


def split_kernel(first, grad_ref, *refs):
    me = lax.axis_index("dp")
    out_ref = refs[-1]
    blocks = [grad_ref[:, k, :] for k in range(grad_ref.shape[1])]
    bit = 1
    while bit < len(blocks):
        flip = (me & bit) != 0
        blocks = [jnp.where(flip, blocks[k ^ bit], blocks[k]) for k in range(len(blocks))]
        bit *= 2
    for k in range(out_ref.shape[0]):
        out_ref[k] = blocks[first + k].T


def split_blocks(out_grad, first, after):
    rows, n, width = out_grad.shape
    step = rows // 4
    return pl.pallas_call(
        functools.partial(split_kernel, first),
        grid=(4,),
        in_specs=[pl.BlockSpec((step, n, width), lambda i: (i, 0, 0))] + [ANY] * len(after),
        out_specs=pl.BlockSpec((n // 2, width, step), lambda i: (0, 0, i)),
        out_shape=jax.ShapeDtypeStruct((n // 2, width, rows), out_grad.dtype),
        compiler_params=pltpu.CompilerParams(vmem_limit_bytes=VMEM),
        name="split_blocks",
    )(out_grad, *after)


def gated(hidden, gate_ref, proj_ref):
    gate = gate_ref[...].T.astype(jnp.float32)
    silu = gate * (0.5 + 0.5 * jnp.tanh(0.5 * gate))
    up_grad = (hidden * silu).astype(jnp.bfloat16)
    return jnp.dot(proj_ref[...], up_grad, preferred_element_type=jnp.float32)


def project_kernel(tiles, ahead, pieces, chained, carried, shard_ref, *refs):
    refs = list(refs)
    take = lambda n: [refs.pop(0) for _ in range(n)]
    grads = take(pieces)
    weights = take(2 * pieces)
    gate_ref, proj_ref = take(2) if tiles else (None, None)
    (before_ref,) = take(1) if chained else (None,)
    (partial_ref,) = take(1) if carried else (None,)
    sum_ref, odd_ref, even_ref = [refs.pop() for _ in range(3)] if tiles else (None,) * 3
    later_ref = refs.pop() if ahead else None
    out_ref = refs.pop() if tiles else None
    step = pl.program_id(0)

    def multiply(hidden_ref):
        hidden = partial_ref[...] if carried else None
        for k, grad_ref in enumerate(grads):
            for p in range(2):
                term = jnp.dot(
                    weights[2 * k + p][...], grad_ref[p], preferred_element_type=jnp.float32
                )
                hidden = term if hidden is None else hidden + term
        hidden_ref[...] = hidden

    if not tiles:
        multiply(later_ref)
        return

    def reduce(hidden_ref):
        sum_ref[...] += gated(hidden_ref[...], gate_ref, proj_ref)

    @pl.when(step == 0)
    def _():
        sum_ref[...] = before_ref[...] if chained else jnp.zeros_like(sum_ref)
        odd_ref[...] = jnp.zeros_like(odd_ref)

    @pl.when((step < tiles) & (lax.rem(step, 2) == 0))
    def _():
        reduce(odd_ref)
        multiply(even_ref)

    if tiles > 1:

        @pl.when((step < tiles) & (lax.rem(step, 2) == 1))
        def _():
            reduce(even_ref)
            multiply(odd_ref)

    @pl.when(step == tiles)
    def _():
        reduce(even_ref if tiles % 2 else odd_ref)
        out_ref[...] = sum_ref[...]

    if ahead:

        @pl.when(step >= tiles)
        def _():
            multiply(later_ref)


def project(shard, grads, gate, weights, proj, offset, span, extra, gate_column, before, partial, after):
    places = [place for place, _ in grads]
    pieces = [piece for _, piece in grads]
    _, width, rows = pieces[0].shape
    count = weights[0].shape[1] // width
    k = proj.shape[0]
    tile = TILE if (span + extra) % TILE == 0 else span + extra
    tiles, ahead = span // tile, extra // tile
    first, gate_first = offset // tile, gate_column // tile
    now = lambda i: jnp.minimum(i, tiles + ahead - 1)
    last = lambda i: jnp.clip(i - 1, 0, max(tiles - 1, 0))
    chained, carried = before is not None, partial is not None
    total = pl.BlockSpec((k, rows), lambda i, s: (0, 0))
    later = pl.BlockSpec((tile, rows), lambda i, s: (jnp.maximum(i - tiles, 0), 0))

    def weight_spec(place):
        return pl.BlockSpec(
            (tile, width), lambda i, s: (first + now(i), lax.rem(s[0] + count - place, count))
        )

    specs = [pl.BlockSpec((2, width, rows), lambda i, s: (0, 0, 0)) for _ in pieces]
    specs += [weight_spec(place) for place in places for _ in range(2)]
    operands = pieces + [weight for _ in places for weight in weights]
    if tiles:
        specs += [
            pl.BlockSpec((rows, tile), lambda i, s: (0, gate_first + last(i))),
            pl.BlockSpec((k, tile), lambda i, s: (0, first + last(i))),
        ]
        operands += [gate, proj]
    if chained:
        specs.append(total)
        operands.append(before)
    if carried:
        specs.append(pl.BlockSpec((tile, rows), lambda i, s: (first + now(i), 0)))
        operands.append(partial)
    hidden = pltpu.VMEM((tile, rows), jnp.float32)
    depth = 2 * width * len(pieces)
    return pl.pallas_call(
        functools.partial(project_kernel, tiles, ahead, len(pieces), chained, carried),
        grid_spec=pltpu.PrefetchScalarGridSpec(
            num_scalar_prefetch=1,
            grid=(tiles + max(ahead, 1) if tiles else ahead,),
            in_specs=specs + [ANY] * len(after),
            out_specs=[total] * bool(tiles) + [later] * bool(ahead),
            scratch_shapes=[hidden, hidden, pltpu.VMEM((k, rows), jnp.float32)] if tiles else [],
        ),
        out_shape=[jax.ShapeDtypeStruct((k, rows), jnp.float32)] * bool(tiles)
        + [jax.ShapeDtypeStruct((extra, rows), jnp.float32)] * bool(ahead),
        compiler_params=pltpu.CompilerParams(vmem_limit_bytes=VMEM),
        cost_estimate=pl.CostEstimate(
            flops=2 * rows * (span + extra) * depth,
            bytes_accessed=2 * (span + extra) * (depth + rows),
            transcendentals=rows * span,
        ),
        name="project",
    )(shard, *operands, *after)


def finish_kernel(hidden_ref, gate_ref, proj_ref, before_ref, *refs):
    out_ref, sum_ref = refs[-2:]
    part = gated(hidden_ref[...], gate_ref, proj_ref)

    @pl.when(pl.program_id(0) == 0)
    def _():
        sum_ref[...] = before_ref[...] + part

    @pl.when(pl.program_id(0) > 0)
    def _():
        sum_ref[...] += part

    @pl.when(pl.program_id(0) == pl.num_programs(0) - 1)
    def _():
        out_ref[...] = sum_ref[...].astype(out_ref.dtype)


def finish(hidden, row, gate, proj, offset, before, dtype, after):
    rows, span = gate.shape
    k = proj.shape[0]
    start, first = row // SMALL, offset // SMALL
    total = pl.BlockSpec((k, rows), lambda i: (0, 0))
    return pl.pallas_call(
        finish_kernel,
        grid=(span // SMALL,),
        in_specs=[
            pl.BlockSpec((SMALL, rows), lambda i: (start + i, 0)),
            pl.BlockSpec((rows, SMALL), lambda i: (0, i)),
            pl.BlockSpec((k, SMALL), lambda i: (0, first + i)),
            total,
        ]
        + [ANY] * len(after),
        out_specs=total,
        out_shape=jax.ShapeDtypeStruct((k, rows), dtype),
        scratch_shapes=[pltpu.VMEM((k, rows), jnp.float32)],
        compiler_params=pltpu.CompilerParams(vmem_limit_bytes=VMEM),
        name="finish",
    )(hidden, gate, proj, before, *after)


def score_kernel(n_both, *refs):
    *parts, query_ref, out_ref = refs
    both = functools.reduce(jnp.add, [ref[...] for ref in parts[:n_both]])
    inputs, grad = jnp.split(both, 2)
    for part_ref in parts[n_both:]:
        grad += part_ref[...].astype(jnp.float32)
    high = grad.astype(jnp.bfloat16)
    low = (grad - high.astype(jnp.float32)).astype(jnp.bfloat16)
    both = jnp.concatenate([high, low], axis=0)
    count = out_ref.shape[0]
    k = inputs.shape[0]
    group = 8
    scores = jnp.zeros(out_ref.shape, jnp.float32)
    for i in range(0, k, group):
        part = jnp.dot(
            query_ref[i * count : (i + group) * count, :], both, preferred_element_type=jnp.float32
        )
        for n in range(group):
            scores += inputs[i + n : i + n + 1, :] * part[n * count : (n + 1) * count, :]
    out_ref[...] = scores


def pair_kernel(k, masks, *refs):
    *block_refs, out_ref = refs
    me = lax.axis_index("dp")
    count, width = block_refs[0].shape
    for mask, block_ref in zip(masks, block_refs):
        base = pl.multiple_of((me ^ mask) * (width // k * count), count)
        for i in range(width // k):
            part = block_ref[:, i * k : (i + 1) * k]
            out_ref[pl.ds(base + i * count, count), :] = jnp.concatenate([part, part], axis=1)


def pair_queries(blocks, masks, k):
    count, width = blocks[0].shape
    return pl.pallas_call(
        functools.partial(pair_kernel, k, masks),
        out_shape=jax.ShapeDtypeStruct((len(blocks) * width // k * count, 2 * k), blocks[0].dtype),
        compiler_params=pltpu.CompilerParams(vmem_limit_bytes=VMEM),
        name="pair_queries",
    )(*blocks)


def score(both, grads, pairs):
    k, rows = grads[0].shape
    return pl.pallas_call(
        functools.partial(score_kernel, len(both)),
        out_shape=jax.ShapeDtypeStruct((pairs.shape[0] // k, rows), jnp.float32),
        compiler_params=pltpu.CompilerParams(vmem_limit_bytes=VMEM),
        name="score",
    )(*both, *grads, pairs)


def chunks_of(hidden):
    units = hidden // TILE
    if hidden % TILE or units < 5:
        return hidden, []
    return hidden - 3 * TILE, [2 * TILE - SMALL, SMALL, TILE]


def on_device(n_dp, n_tensor, inputs, out_grad, gate_pre, down_weight, proj_in, proj_out, queries):
    rows = out_grad.shape[0]
    hidden = gate_pre.shape[1]
    me = lax.axis_index("dp")
    shard = lax.axis_index("tensor").astype(jnp.int32).reshape(1)
    far, near = n_dp // 2, 1
    ring = n_tensor <= RING
    main, spans = chunks_of(hidden)
    offsets = [main + sum(spans[:k]) for k in range(len(spans))]

    def onward(piece, hold=None):
        if hold is not None:
            piece, _ = lax.optimization_barrier((piece, hold))
        return lax.ppermute(piece, "tensor", [(i, (i + 1) % n_tensor) for i in range(n_tensor)])

    def gather(block):
        grad = lax.all_gather(block, "tensor", axis=0, tiled=False)
        return jnp.transpose(grad, (1, 0, 2, 3)).reshape(2, -1, rows)

    def spread(value, mask):
        if not ring:
            total = lax.psum(value.astype(jnp.float32), "tensor")
            return [swap(total, "dp", n_dp, mask) if mask else total]
        got = [value] if not mask else []
        for step in range(0 if mask else 1, n_tensor):
            pairs = [
                (z * n_dp + d, (z + step) % n_tensor * n_dp + (d ^ mask))
                for z in range(n_tensor)
                for d in range(n_dp)
            ]
            got.append(lax.ppermute(value, ("tensor", "dp"), pairs))
        return got

    weights = (down_weight, swap(down_weight, "dp", n_dp, near))

    cut = lambda source, offset, span: source[:, offset : offset + span]
    start_gate = cut(gate_pre, offsets[-1], spans[-1]) if spans else None
    own_blocks = split_blocks(out_grad, 0, (start_gate,) if spans else ())
    far_blocks = split_blocks(out_grad, n_dp // 2, (own_blocks,))
    if spans:
        start_gate = swap(start_gate, "dp", n_dp, far)
    far_query = swap(queries, "dp", n_dp, far)
    later_gate, _ = lax.optimization_barrier((gate_pre, own_blocks))
    parts = [cut(later_gate, 0, main)]
    parts += [cut(later_gate, offset, span) for offset, span in zip(offsets[:-1], spans)]
    far_blocks, start_gate, parts, _ = lax.optimization_barrier(
        (far_blocks, start_gate, parts, far_query)
    )
    far_start = swap(far_blocks, "dp", n_dp, far)
    own = [own_blocks, onward(own_blocks)] if ring and n_tensor > 1 else [own_blocks]
    parts, _ = lax.optimization_barrier((parts, own[-1]))
    far_gate, *last_gates = [swap(part, "dp", n_dp, far) for part in parts]

    def all_pairs(hold):
        blocks, _ = lax.optimization_barrier(((queries, far_query), hold))
        blocks += tuple(swap(block, "dp", n_dp, near) for block in blocks)
        return pair_queries(blocks, (0, far, near, far ^ near), proj_in.shape[1])

    proj_out = proj_out.T
    if ring and n_tensor > 1:
        split = n_tensor // 2
        while len(own) <= split:
            own.append(onward(own[-1]))
        own_early = list(enumerate(own))[:split]
        middle = hidden // (2 * TILE) * TILE if hidden % TILE == 0 else 0
        halves = [(s, n) for s, n in ((0, middle), (middle, hidden - middle)) if n]
        own_sum, after = None, ()
        for s, span in halves:
            (own_sum,) = project(
                shard, own_early, gate_pre, weights, proj_out, s, span, 0, s, own_sum, None, after
            )
            if s == 0:
                first_sum = own_sum
            after = (own[-1],)
        early_sum = own_sum
        pairs = all_pairs(early_sum)
        others = [far_start]
        for _ in range(split - 1):
            others.append(onward(others[-1], first_sum))
        far_early = list(enumerate(others))
        (partial,) = project(
            shard, far_early, None, weights, proj_out, 0, 0, hidden, 0, None, None, (own_sum,)
        )
        while len(own) < n_tensor:
            own.append(onward(own[-1], first_sum))
        own_late = list(enumerate(own))[split:]
        after = (partial,)
        for s, span in halves:
            (own_sum,) = project(
                shard, own_late, gate_pre, weights, proj_out, s, span, 0, s, own_sum, None, after
            )
            if s == 0:
                while len(others) < n_tensor:
                    hold = own_sum if len(others) == n_tensor - 1 else early_sum
                    others.append(onward(others[-1], hold))
            after = (pairs, others[-2])
        far_late = list(enumerate(others))[split:]
    else:
        (own_sum,) = project(
            shard, [(0, gather(own_blocks))], gate_pre, weights, proj_out, 0, hidden, 0, 0, None, None, ()
        )
        far_late, partial = [(0, gather(far_start))], None
        pairs = all_pairs(own_sum)

    input_part = lax.dot_general(
        proj_in, inputs, (((0,), (1,)), ((), ())), preferred_element_type=jnp.float32
    )
    both = jnp.concatenate([input_part, own_sum])
    both, far_gate = lax.optimization_barrier((both, far_gate))
    terms = spread(both, 0)

    far_sum, *later = project(
        shard, far_late, far_gate, weights, proj_out, 0, main, sum(spans), 0, None, partial, (own_sum,)
    )
    if later:
        order = [len(spans) - 1] + list(range(len(spans) - 1))
        for k, gate in zip(order, [start_gate] + last_gates):
            final = k == order[-1]
            far_sum = finish(
                later[0],
                offsets[k] - main,
                gate,
                proj_out,
                offsets[k],
                far_sum,
                jnp.bfloat16 if final else jnp.float32,
                tuple(terms[1:]) if final else (),
            )
    return score(terms, spread(far_sum, far), pairs)


def solution(mesh):
    return jax.shard_map(
        functools.partial(on_device, mesh.shape["dp"], mesh.shape["tensor"]),
        mesh=mesh,
        in_specs=(
            P(("parts", "dp"), "tensor"),
            P(("parts", "dp"), None, "tensor"),
            P(("parts", "dp"), "tensor"),
            P("tensor", "dp"),
            P("tensor", None),
            P("tensor", None),
            P("tensor", "dp"),
        ),
        out_specs=P("tensor", ("parts", "dp")),
        check_vma=False,
    )
```

profile of v0, /device:TPU:0, one launch (start us, length us, event | category | flops | bytes accessed | tf_op | source)
XLA Modules:
  0.0 217.7 jit_solution(7926605167262348109)
XLA Ops:
  0.0 0.5 collective-permute-start.2
  0.5 1.5 slice.12.refs_0_
  1.9 2.5 %collective-permute-start.4 = (bf16[512,1024]{1,0:T(8,128)(2,1)S(1)}, bf16[512,1024]{1,0:T(8,128)(2,1)}, u32[]{:S(2)}, u32[]{:S(2)}) collective-permute-start(bf16[512,1024]{1,0:T(8,128)(2,1)S(1)} %slice.12.refs_0_), channel_id=1, source_target_pairs={{0,2},{1,3},{2,0},{3,1},{4,6},{5,7},{6,4},{7,5},{8,10},{9,11},{10,... | collective-permute-start | bytes 3145736 | tf_op jit(solution)/shard_map/ppermute | solution.py:18
  4.5 5.4 %split_blocks.2.refs_0_ = bf16[2,512,512]{2,1,0:T(8,128)(2,1)} custom-call(bf16[512,4,512]{2,1,0:T(4,128)(2,1)} %grad_ref.3, bf16[512,1024]{1,0:T(8,128)(2,1)} %copy-done.2), custom_call_target="tpu_custom_call" | custom-call | tf_op jit(solution)/shard_map/split_blocks/pallas_call | solution.py:37
  9.9 1.6 collective-permute-start
  11.4 0.9 collective-permute-start.5
  12.4 4.7 %slice.13 = bf16[512,4096]{1,0:T(8,128)(2,1)} slice(bf16[512,7168]{1,0:T(8,128)(2,1)} %refs_6_.7), slice={[0:512], [0:4096]} | slice | bytes 8388608 | tf_op jit(solution)/shard_map/slice | solution.py:307
  17.1 2.7 %slice.14 = bf16[512,1536]{1,0:T(8,128)(2,1)} slice(bf16[512,7168]{1,0:T(8,128)(2,1)} %refs_6_.7), slice={[0:512], [4096:5632]} | slice | bytes 3145728 | tf_op jit(solution)/shard_map/slice | solution.py:307
  19.8 1.9 slice.15
  21.7 5.4 %split_blocks.3 = bf16[2,512,512]{2,1,0:T(8,128)(2,1)} custom-call(bf16[512,4,512]{2,1,0:T(4,128)(2,1)} %grad_ref.3, bf16[2,512,512]{2,1,0:T(8,128)(2,1)} %split_blocks.2.refs_0_), custom_call_target="tpu_custom_call" | custom-call | tf_op jit(solution)/shard_map/split_blocks/pallas_call | solution.py:37
  27.0 4.0 %collective-permute-done.5.refs_1_ = bf16[64,1024]{1,0:T(8,128)(2,1)} collective-permute-done((bf16[64,1024]{1,0:T(8,128)(2,1)}, bf16[64,1024]{1,0:T(8,128)(2,1)}, u32[]{:S(2)}, u32[]{:S(2)}) %collective-permute-start.5) | collective-permute-done | bytes 131104 | tf_op jit(solution)/shard_map/ppermute | solution.py:18
  31.1 0.0 collective-permute-done.4.gate_ref
  31.1 1.7 collective-permute-start.6
  32.8 4.4 %collective-permute-done.refs_1_ = bf16[2,512,512]{2,1,0:T(8,128)(2,1)} collective-permute-done((bf16[2,512,512]{2,1,0:T(8,128)(2,1)}, bf16[2,512,512]{2,1,0:T(8,128)(2,1)}, u32[]{:S(2)}, u32[]{:S(2)}) %collective-permute-start) | collective-permute-done | bytes 1048608 | tf_op jit(solution)/shard_map/ppermute | solution.py:285
  37.2 0.0 collective-permute-start.1
  37.2 6.4 %collective-permute-done.2.refs_3_.refs_5_ = bf16[7168,2048]{1,0:T(8,128)(2,1)} collective-permute-done((bf16[7168,2048]{1,0:T(8,128)(2,1)}, bf16[7168,2048]{1,0:T(8,128)(2,1)}, u32[]{:S(2)}, u32[]{:S(2)}) %collective-permute-start.2) | collective-permute-done | bytes 29360160 | tf_op jit(solution)/shard_map/ppermute | solution.py:18
  43.6 14.7 %project.6.refs_8_ = f32[64,512]{1,0:T(8,128)} custom-call(s32[1]{0:T(128)} %bitcast.shard_ref, bf16[2,512,512]{2,1,0:T(8,128)(2,1)} %split_blocks.2.refs_0_, bf16[2,512,512]{2,1,0:T(8,128)(2,1)} %collective-permute-done.refs_1_, bf16[7168,2048]{1,0:T(8,128)(2,1)} %refs_4_.11, bf16[7168,2048]{1,0:T(8,128)(2,1)} %collective-permute-done.2.refs_3_.refs_5_, ...), custom_call_target="tpu_custom_call" | custom-call | flops 6442450944 | bytes 15728640 | tf_op jit(solution)/shard_map/project/pallas_call | solution.py:151
  58.3 0.0 collective-permute-done.6.refs_0_
  58.3 3.0 %collective-permute-start.7 = (bf16[2,512,512]{2,1,0:T(8,128)(2,1)}, bf16[2,512,512]{2,1,0:T(8,128)(2,1)}, u32[]{:S(2)}, u32[]{:S(2)}) collective-permute-start(bf16[2,512,512]{2,1,0:T(8,128)(2,1)} %collective-permute-done.6.refs_0_), channel_id=1, source_target_pairs={{0,4},{4,8},{8,12},{12,0},{1,5},{5,9},{9,13},{13,1},{2,6},{6,10},{... | collective-permute-start | bytes 3145736 | tf_op jit(solution)/shard_map/ppermute | solution.py:285
  61.3 1.5 collective-permute-start.11
  62.8 0.8 collective-permute-done.1.refs_9_.refs_0_
  63.6 0.8 collective-permute-start.3
  64.4 0.2 copy-done.1
  64.6 17.8 %project.7.refs_6_.refs_8_ = f32[64,512]{1,0:T(8,128)} custom-call(s32[1]{0:T(128)} %bitcast.shard_ref, bf16[2,512,512]{2,1,0:T(8,128)(2,1)} %split_blocks.2.refs_0_, bf16[2,512,512]{2,1,0:T(8,128)(2,1)} %collective-permute-done.refs_1_, bf16[7168,2048]{1,0:T(8,128)(2,1)} %refs_4_.11, bf16[7168,2048]{1,0:T(8,128)(2,1)} %collective-permute-done.2.refs_3_.refs_5_, ...), custom_call_target="tpu_custom_call" | custom-call | flops 8589934592 | bytes 20971520 | tf_op jit(solution)/shard_map/project/pallas_call | solution.py:151
  82.4 0.0 collective-permute-start.8
  82.4 0.5 collective-permute-start.9
  82.9 4.7 %collective-permute-done.7.refs_1_ = bf16[2,512,512]{2,1,0:T(8,128)(2,1)} collective-permute-done((bf16[2,512,512]{2,1,0:T(8,128)(2,1)}, bf16[2,512,512]{2,1,0:T(8,128)(2,1)}, u32[]{:S(2)}, u32[]{:S(2)}) %collective-permute-start.7) | collective-permute-done | bytes 1048608 | tf_op jit(solution)/shard_map/ppermute | solution.py:285
  87.6 0.0 collective-permute-start.10
  87.6 22.8 %project.8.refs_9_.refs_8_ = f32[7168,512]{1,0:T(8,128)} custom-call(s32[1]{0:T(128)} %bitcast.shard_ref, bf16[2,512,512]{2,1,0:T(8,128)(2,1)} %collective-permute-done.6.refs_0_, bf16[2,512,512]{2,1,0:T(8,128)(2,1)} %collective-permute-done.7.refs_1_, bf16[7168,2048]{1,0:T(8,128)(2,1)} %refs_4_.11, ...), custom_call_target="tpu_custom_call" | custom-call | flops 15032385536 | bytes 36700160 | tf_op jit(solution)/shard_map/project/pallas_call | solution.py:151
  110.4 0.0 collective-permute-done.3.refs_1_
  110.4 14.9 %project.9.refs_8_ = f32[64,512]{1,0:T(8,128)} custom-call(s32[1]{0:T(128)} %bitcast.shard_ref, bf16[2,512,512]{2,1,0:T(8,128)(2,1)} %copy-done.1, bf16[2,512,512]{2,1,0:T(8,128)(2,1)} %collective-permute-done.3.refs_1_, bf16[7168,2048]{1,0:T(8,128)(2,1)} %refs_4_.11, bf16[7168,2048]{1,0:T(8,128)(2,1)} %collective-permute-done.2.refs_3_.refs_5_, ...), custom_call_target="tpu_custom_call" | custom-call | flops 6442450944 | bytes 15728640 | tf_op jit(solution)/shard_map/project/pallas_call | solution.py:151
  125.3 6.7 %collective-permute-done.10.refs_10_.refs_0_ = bf16[2,512,512]{2,1,0:T(8,128)(2,1)} collective-permute-done((bf16[2,512,512]{2,1,0:T(8,128)(2,1)}, bf16[2,512,512]{2,1,0:T(8,128)(2,1)}, u32[]{:S(2)}, u32[]{:S(2)}) %collective-permute-start.10) | collective-permute-done | bytes 1048608 | tf_op jit(solution)/shard_map/ppermute | solution.py:285
  132.0 0.0 collective-permute-start.15
  132.0 0.8 fusion
  132.8 1.6 collective-permute-start.17
  134.3 0.0 collective-permute-done.8.refs_2_
  134.3 0.5 collective-permute-start.16
  134.9 0.0 collective-permute-done.9.refs_3_
  134.9 2.4 %pair_queries.1.refs_9_.refs_8_ = bf16[4096,128]{1,0:T(8,128)(2,1)} custom-call(bf16[64,1024]{1,0:T(8,128)(2,1)} %refs_0_, bf16[64,1024]{1,0:T(8,128)(2,1)} %collective-permute-done.5.refs_1_, bf16[64,1024]{1,0:T(8,128)(2,1)} %collective-permute-done.8.refs_2_, bf16[64,1024]{1,0:T(8,128)(2,1)} %collective-permute-done.9.refs_3_), custom_call_target="tpu_custom_call" | custom-call | tf_op jit(solution)/shard_map/pair_queries/pallas_call | solution.py:247
  137.3 17.8 %project.10.refs_9_ = f32[64,512]{1,0:T(8,128)} custom-call(s32[1]{0:T(128)} %bitcast.shard_ref, bf16[2,512,512]{2,1,0:T(8,128)(2,1)} %copy-done.1, bf16[2,512,512]{2,1,0:T(8,128)(2,1)} %collective-permute-done.3.refs_1_, bf16[7168,2048]{1,0:T(8,128)(2,1)} %refs_4_.11, bf16[7168,2048]{1,0:T(8,128)(2,1)} %collective-permute-done.2.refs_3_.refs_5_, ...), custom_call_target="tpu_custom_call" | custom-call | flops 8589934592 | bytes 20971520 | tf_op jit(solution)/shard_map/project/pallas_call | solution.py:151
  155.1 1.6 pad_maximum_fusion.refs_0_
  156.7 0.0 collective-permute-done.11.refs_6_
  156.7 1.3 collective-permute-start.12
  158.0 3.1 %collective-permute-start.13 = (f32[128,512]{1,0:T(8,128)}, f32[128,512]{1,0:T(8,128)}, u32[]{:S(2)}, u32[]{:S(2)}) collective-permute-start(f32[128,512]{1,0:T(8,128)} %pad_maximum_fusion.refs_0_), channel_id=1, source_target_pairs={{0,8},{1,9},{2,10},{3,11},{4,12},{5,13},{6,14},{7,15},{8,0},{9,1},... | collective-permute-start | bytes 786440 | tf_op jit(solution)/shard_map/ppermute | solution.py:302
  161.1 0.0 collective-permute-done.15.refs_1_
  161.1 0.8 collective-permute-start.14
  162.0 28.1 %project.11 = (f32[64,512]{1,0:T(8,128)}, f32[3072,512]{1,0:T(8,128)}) custom-call(s32[1]{0:T(128)} %bitcast.shard_ref, bf16[2,512,512]{2,1,0:T(8,128)(2,1)} %collective-permute-done.10.refs_10_.refs_0_, bf16[2,512,512]{2,1,0:T(8,128)(2,1)} %collective-permute-done.15.refs_1_, bf16[7168,2048]{1,0:T(8,128)(2,1)} %refs_4_.11, ...), custom_call_target="tpu_custom_call" | custom-call | flops 15032385536 | bytes 36700160 | tf_op jit(solution)/shard_map/project/pallas_call | solution.py:151
  190.1 3.2 %finish.3.before_ref = f32[64,512]{1,0:T(8,128)} custom-call(f32[3072,512]{1,0:T(8,128)} %get-tuple-element.38.hidden_ref, bf16[512,1024]{1,0:T(8,128)(2,1)} %collective-permute-done.4.gate_ref, bf16[64,7168]{1,0:T(8,128)(2,1)} %bitcast.9, f32[64,512]{1,0:T(8,128)} %get-tuple-element.42.before_ref), custom_call_target="tpu_custom_call" | custom-call | tf_op jit(solution)/shard_map/finish/pallas_call | solution.py:194
  193.3 4.9 %finish.4.before_ref = f32[64,512]{1,0:T(8,128)} custom-call(f32[3072,512]{1,0:T(8,128)} %get-tuple-element.38.hidden_ref, bf16[512,1536]{1,0:T(8,128)(2,1)} %collective-permute-done.17.gate_ref, bf16[64,7168]{1,0:T(8,128)(2,1)} %bitcast.10, f32[64,512]{1,0:T(8,128)} %finish.3.before_ref), custom_call_target="tpu_custom_call" | custom-call | tf_op jit(solution)/shard_map/finish/pallas_call | solution.py:194
  198.3 0.6 collective-permute-done.16.gate_ref
  198.9 0.0 collective-permute-done.13.refs_1_.refs_2_
  198.9 0.0 collective-permute-done.14.refs_2_.refs_3_
  198.9 0.7 copy-done.4
  199.6 2.5 %finish.5 = bf16[64,512]{1,0:T(8,128)(2,1)} custom-call(f32[3072,512]{1,0:T(8,128)} %get-tuple-element.38.hidden_ref, bf16[512,512]{1,0:T(8,128)(2,1)} %collective-permute-done.16.gate_ref, bf16[64,7168]{1,0:T(8,128)(2,1)} %bitcast.11, f32[64,512]{1,0:T(8,128)} %finish.4.before_ref, f32[128,512]{1,0:T(8,128)} %copy-done.4, ...), custom_call_target="tpu_custom_call" | custom-call | tf_op jit(solution)/shard_map/finish/pallas_call | solution.py:194
  202.1 1.5 collective-permute-start.18
  203.6 1.6 collective-permute-start.19
  205.1 2.3 %collective-permute-start.20 = (bf16[64,512]{1,0:T(8,128)(2,1)}, bf16[64,512]{1,0:T(8,128)(2,1)S(1)}, u32[]{:S(2)}, u32[]{:S(2)}) collective-permute-start(bf16[64,512]{1,0:T(8,128)(2,1)} %finish.5), channel_id=1, source_target_pairs={{0,10},{1,11},{2,8},{3,9},{4,14},{5,15},{6,12},{7,13},{8,2},{9,3},... | collective-permute-start | bytes 196616 | tf_op jit(solution)/shard_map/ppermute | solution.py:302
  207.4 2.5 %collective-permute-start.21 = (bf16[64,512]{1,0:T(8,128)(2,1)}, bf16[64,512]{1,0:T(8,128)(2,1)S(1)}, u32[]{:S(2)}, u32[]{:S(2)}) collective-permute-start(bf16[64,512]{1,0:T(8,128)(2,1)} %finish.5), channel_id=1, source_target_pairs={{0,14},{1,15},{2,12},{3,13},{4,2},{5,3},{6,0},{7,1},{8,6},{9,7},{1... | collective-permute-start | bytes 196616 | tf_op jit(solution)/shard_map/ppermute | solution.py:302
  210.0 1.2 collective-permute-done.19.refs_5_
  211.2 1.8 collective-permute-done.20.refs_6_
  212.9 0.1 collective-permute-done.21.refs_7_
  213.1 0.5 copy-done.8
  213.6 0.6 copy-done.9
  214.2 3.6 %score.1 = f32[64,512]{1,0:T(8,128)} custom-call(f32[128,512]{1,0:T(8,128)} %pad_maximum_fusion.refs_0_, f32[128,512]{1,0:T(8,128)} %copy-done.4, f32[128,512]{1,0:T(8,128)} %collective-permute-done.13.refs_1_.refs_2_, f32[128,512]{1,0:T(8,128)} %collective-permute-done.14.refs_2_.refs_3_, bf16[64,512]{1,0:T(8,128)(2,1)} %copy-done.6, ...), custom_call_target="tpu_custom_call" | custom-call | tf_op jit(solution)/shard_map/score/pallas_call | solution.py:257
  (19 shorter events, 0.0 us)
Async XLA Ops:
  0.0 132.0 %copy-start = (bf16[512,2048]{1,0:T(8,128)(2,1)S(1)}, bf16[512,2048]{1,0:T(8,128)(2,1)}, u32[]{:S(2)}) copy-start(bf16[512,2048]{1,0:T(8,128)(2,1)} %param.7) | copy-start | bytes 6291460
  0.0 43.6 %collective-permute-start.2 = (bf16[7168,2048]{1,0:T(8,128)(2,1)}, bf16[7168,2048]{1,0:T(8,128)(2,1)}, u32[]{:S(2)}, u32[]{:S(2)}) collective-permute-start(bf16[7168,2048]{1,0:T(8,128)(2,1)} %refs_4_.11), channel_id=1, source_target_pairs={{0,1},{1,0},{2,3},{3,2},{4,5},{5,4},{6,7},{7,6},{8,9},{9,8},{10,11... | collective-permute-start | bytes 88080392 | tf_op jit(solution)/shard_map/ppermute | solution.py:18
  1.9 2.5 %copy-start.2 = (bf16[512,1024]{1,0:T(8,128)(2,1)}, bf16[512,1024]{1,0:T(8,128)(2,1)S(1)}, u32[]{:S(2)}) copy-start(bf16[512,1024]{1,0:T(8,128)(2,1)S(1)} %slice.12.refs_0_) | copy-start | bytes 3145732
  1.9 29.1 %collective-permute-start.4 = (bf16[512,1024]{1,0:T(8,128)(2,1)S(1)}, bf16[512,1024]{1,0:T(8,128)(2,1)}, u32[]{:S(2)}, u32[]{:S(2)}) collective-permute-start(bf16[512,1024]{1,0:T(8,128)(2,1)S(1)} %slice.12.refs_0_), channel_id=1, source_target_pairs={{0,2},{1,3},{2,0},{3,1},{4,6},{5,7},{6,4},{7,5},{8,10},{9,11},{10,... | collective-permute-start | bytes 3145736 | tf_op jit(solution)/shard_map/ppermute | solution.py:18
  9.9 27.3 %collective-permute-start = (bf16[2,512,512]{2,1,0:T(8,128)(2,1)}, bf16[2,512,512]{2,1,0:T(8,128)(2,1)}, u32[]{:S(2)}, u32[]{:S(2)}) collective-permute-start(bf16[2,512,512]{2,1,0:T(8,128)(2,1)} %split_blocks.2.refs_0_), channel_id=1, source_target_pairs={{0,4},{4,8},{8,12},{12,0},{1,5},{5,9},{9,13},{13,1},{2,6},{6,10},{... | collective-permute-start | bytes 3145736 | tf_op jit(solution)/shard_map/ppermute | solution.py:285
  11.4 19.6 %collective-permute-start.5 = (bf16[64,1024]{1,0:T(8,128)(2,1)}, bf16[64,1024]{1,0:T(8,128)(2,1)}, u32[]{:S(2)}, u32[]{:S(2)}) collective-permute-start(bf16[64,1024]{1,0:T(8,128)(2,1)} %refs_0_), channel_id=1, source_target_pairs={{0,2},{1,3},{2,0},{3,1},{4,6},{5,7},{6,4},{7,5},{8,10},{9,11},{10,... | collective-permute-start | bytes 393224 | tf_op jit(solution)/shard_map/ppermute | solution.py:18
  31.1 27.2 %collective-permute-start.6 = (bf16[2,512,512]{2,1,0:T(8,128)(2,1)}, bf16[2,512,512]{2,1,0:T(8,128)(2,1)}, u32[]{:S(2)}, u32[]{:S(2)}) collective-permute-start(bf16[2,512,512]{2,1,0:T(8,128)(2,1)} %split_blocks.3), channel_id=1, source_target_pairs={{0,2},{1,3},{2,0},{3,1},{4,6},{5,7},{6,4},{7,5},{8,10},{9,11},{10,... | collective-permute-start | bytes 3145736 | tf_op jit(solution)/shard_map/ppermute | solution.py:18
  37.2 26.4 %collective-permute-start.1 = (bf16[2,512,512]{2,1,0:T(8,128)(2,1)}, bf16[2,512,512]{2,1,0:T(8,128)(2,1)S(1)}, u32[]{:S(2)}, u32[]{:S(2)}) collective-permute-start(bf16[2,512,512]{2,1,0:T(8,128)(2,1)} %collective-permute-done.refs_1_), channel_id=1, source_target_pairs={{0,4},{4,8},{8,12},{12,0},{1,5},{5,9},{9,13},{13,1},{2,6},{6,10},{... | collective-permute-start | bytes 3145736 | tf_op jit(solution)/shard_map/ppermute | solution.py:285
  58.3 29.3 %collective-permute-start.7 = (bf16[2,512,512]{2,1,0:T(8,128)(2,1)}, bf16[2,512,512]{2,1,0:T(8,128)(2,1)}, u32[]{:S(2)}, u32[]{:S(2)}) collective-permute-start(bf16[2,512,512]{2,1,0:T(8,128)(2,1)} %collective-permute-done.6.refs_0_), channel_id=1, source_target_pairs={{0,4},{4,8},{8,12},{12,0},{1,5},{5,9},{9,13},{13,1},{2,6},{6,10},{... | collective-permute-start | bytes 3145736 | tf_op jit(solution)/shard_map/ppermute | solution.py:285
  61.3 95.5 %collective-permute-start.11 = (bf16[512,4096]{1,0:T(8,128)(2,1)}, bf16[512,4096]{1,0:T(8,128)(2,1)}, u32[]{:S(2)}, u32[]{:S(2)}) collective-permute-start(bf16[512,4096]{1,0:T(8,128)(2,1)} %slice.13), channel_id=1, source_target_pairs={{0,2},{1,3},{2,0},{3,1},{4,6},{5,7},{6,4},{7,5},{8,10},{9,11},{10,... | collective-permute-start | bytes 12582920 | tf_op jit(solution)/shard_map/ppermute | solution.py:18
  63.6 1.0 copy-start.1
  63.6 46.9 %collective-permute-start.3 = (bf16[2,512,512]{2,1,0:T(8,128)(2,1)S(1)}, bf16[2,512,512]{2,1,0:T(8,128)(2,1)}, u32[]{:S(2)}, u32[]{:S(2)}) collective-permute-start(bf16[2,512,512]{2,1,0:T(8,128)(2,1)S(1)} %collective-permute-done.1.refs_9_.refs_0_), channel_id=1, source_target_pairs={{0,4},{4,8},{8,12},{12,0},{1,5},{5,9},{9,13},{13,1},{2,6},{6,10},{... | collective-permute-start | bytes 3145736 | tf_op jit(solution)/shard_map/ppermute | solution.py:285
  82.4 52.0 %collective-permute-start.8 = (bf16[64,1024]{1,0:T(8,128)(2,1)}, bf16[64,1024]{1,0:T(8,128)(2,1)}, u32[]{:S(2)}, u32[]{:S(2)}) collective-permute-start(bf16[64,1024]{1,0:T(8,128)(2,1)} %refs_0_), channel_id=1, source_target_pairs={{0,1},{1,0},{2,3},{3,2},{4,5},{5,4},{6,7},{7,6},{8,9},{9,8},{10,11... | collective-permute-start | bytes 393224 | tf_op jit(solution)/shard_map/ppermute | solution.py:18
  82.4 52.5 %collective-permute-start.9 = (bf16[64,1024]{1,0:T(8,128)(2,1)}, bf16[64,1024]{1,0:T(8,128)(2,1)}, u32[]{:S(2)}, u32[]{:S(2)}) collective-permute-start(bf16[64,1024]{1,0:T(8,128)(2,1)} %collective-permute-done.5.refs_1_), channel_id=1, source_target_pairs={{0,1},{1,0},{2,3},{3,2},{4,5},{5,4},{6,7},{7,6},{8,9},{9,8},{10,11... | collective-permute-start | bytes 393224 | tf_op jit(solution)/shard_map/ppermute | solution.py:18
  87.6 44.5 %collective-permute-start.10 = (bf16[2,512,512]{2,1,0:T(8,128)(2,1)}, bf16[2,512,512]{2,1,0:T(8,128)(2,1)}, u32[]{:S(2)}, u32[]{:S(2)}) collective-permute-start(bf16[2,512,512]{2,1,0:T(8,128)(2,1)} %collective-permute-done.7.refs_1_), channel_id=1, source_target_pairs={{0,4},{4,8},{8,12},{12,0},{1,5},{5,9},{9,13},{13,1},{2,6},{6,10},{... | collective-permute-start | bytes 3145736 | tf_op jit(solution)/shard_map/ppermute | solution.py:285
  110.4 21.6 %copy-start.5 = (bf16[2048,64]{0,1:T(8,128)(2,1)S(1)}, bf16[2048,64]{0,1:T(8,128)(2,1)}, u32[]{:S(2)}) copy-start(bf16[2048,64]{0,1:T(8,128)(2,1)} %param.11) | copy-start | bytes 786436
  110.4 22.3 %copy-start.3 = (bf16[512,1536]{1,0:T(8,128)(2,1)S(1)}, bf16[512,1536]{1,0:T(8,128)(2,1)}, u32[]{:S(2)}) copy-start(bf16[512,1536]{1,0:T(8,128)(2,1)} %slice.14) | copy-start | bytes 4718596
  132.0 29.1 %collective-permute-start.15 = (bf16[2,512,512]{2,1,0:T(8,128)(2,1)}, bf16[2,512,512]{2,1,0:T(8,128)(2,1)}, u32[]{:S(2)}, u32[]{:S(2)}) collective-permute-start(bf16[2,512,512]{2,1,0:T(8,128)(2,1)} %collective-permute-done.10.refs_10_.refs_0_), channel_id=1, source_target_pairs={{0,4},{4,8},{8,12},{12,0},{1,5},{5,9},{9,13},{13,1},{2,6},{6,10},{... | collective-permute-start | bytes 3145736 | tf_op jit(solution)/shard_map/ppermute | solution.py:285
  132.8 60.5 %collective-permute-start.17 = (bf16[512,1536]{1,0:T(8,128)(2,1)S(1)}, bf16[512,1536]{1,0:T(8,128)(2,1)}, u32[]{:S(2)}, u32[]{:S(2)}) collective-permute-start(bf16[512,1536]{1,0:T(8,128)(2,1)S(1)} %copy-done.3), channel_id=1, source_target_pairs={{0,2},{1,3},{2,0},{3,1},{4,6},{5,7},{6,4},{7,5},{8,10},{9,11},{10,... | collective-permute-start | bytes 4718600 | tf_op jit(solution)/shard_map/ppermute | solution.py:18
  134.3 64.5 %collective-permute-start.16 = (bf16[512,512]{1,0:T(8,128)(2,1)}, bf16[512,512]{1,0:T(8,128)(2,1)}, u32[]{:S(2)}, u32[]{:S(2)}) collective-permute-start(bf16[512,512]{1,0:T(8,128)(2,1)} %slice.15), channel_id=1, source_target_pairs={{0,2},{1,3},{2,0},{3,1},{4,6},{5,7},{6,4},{7,5},{8,10},{9,11},{10,... | collective-permute-start | bytes 1572872 | tf_op jit(solution)/shard_map/ppermute | solution.py:18
  156.7 42.1 %collective-permute-start.12 = (f32[128,512]{1,0:T(8,128)}, f32[128,512]{1,0:T(8,128)S(1)}, u32[]{:S(2)}, u32[]{:S(2)}) collective-permute-start(f32[128,512]{1,0:T(8,128)} %pad_maximum_fusion.refs_0_), channel_id=1, source_target_pairs={{0,4},{1,5},{2,6},{3,7},{4,8},{5,9},{6,10},{7,11},{8,12},{9,13},{1... | collective-permute-start | bytes 786440 | tf_op jit(solution)/shard_map/ppermute | solution.py:302
  158.0 40.8 %collective-permute-start.13 = (f32[128,512]{1,0:T(8,128)}, f32[128,512]{1,0:T(8,128)}, u32[]{:S(2)}, u32[]{:S(2)}) collective-permute-start(f32[128,512]{1,0:T(8,128)} %pad_maximum_fusion.refs_0_), channel_id=1, source_target_pairs={{0,8},{1,9},{2,10},{3,11},{4,12},{5,13},{6,14},{7,15},{8,0},{9,1},... | collective-permute-start | bytes 786440 | tf_op jit(solution)/shard_map/ppermute | solution.py:302
  161.1 37.7 %collective-permute-start.14 = (f32[128,512]{1,0:T(8,128)}, f32[128,512]{1,0:T(8,128)}, u32[]{:S(2)}, u32[]{:S(2)}) collective-permute-start(f32[128,512]{1,0:T(8,128)} %pad_maximum_fusion.refs_0_), channel_id=1, source_target_pairs={{0,12},{1,13},{2,14},{3,15},{4,0},{5,1},{6,2},{7,3},{8,4},{9,5},{1... | collective-permute-start | bytes 786440 | tf_op jit(solution)/shard_map/ppermute | solution.py:302
  198.9 0.7 copy-start.4
  202.1 7.9 %collective-permute-start.18 = (bf16[64,512]{1,0:T(8,128)(2,1)}, bf16[64,512]{1,0:T(8,128)(2,1)S(1)}, u32[]{:S(2)}, u32[]{:S(2)}) collective-permute-start(bf16[64,512]{1,0:T(8,128)(2,1)} %finish.5), channel_id=1, source_target_pairs={{0,2},{1,3},{2,0},{3,1},{4,6},{5,7},{6,4},{7,5},{8,10},{9,11},{10,... | collective-permute-start | bytes 196616 | tf_op jit(solution)/shard_map/ppermute | solution.py:302
  203.6 7.6 %collective-permute-start.19 = (bf16[64,512]{1,0:T(8,128)(2,1)}, bf16[64,512]{1,0:T(8,128)(2,1)S(1)}, u32[]{:S(2)}, u32[]{:S(2)}) collective-permute-start(bf16[64,512]{1,0:T(8,128)(2,1)} %finish.5), channel_id=1, source_target_pairs={{0,6},{1,7},{2,4},{3,5},{4,10},{5,11},{6,8},{7,9},{8,14},{9,15},{1... | collective-permute-start | bytes 196616 | tf_op jit(solution)/shard_map/ppermute | solution.py:302
  205.1 7.8 %collective-permute-start.20 = (bf16[64,512]{1,0:T(8,128)(2,1)}, bf16[64,512]{1,0:T(8,128)(2,1)S(1)}, u32[]{:S(2)}, u32[]{:S(2)}) collective-permute-start(bf16[64,512]{1,0:T(8,128)(2,1)} %finish.5), channel_id=1, source_target_pairs={{0,10},{1,11},{2,8},{3,9},{4,14},{5,15},{6,12},{7,13},{8,2},{9,3},... | collective-permute-start | bytes 196616 | tf_op jit(solution)/shard_map/ppermute | solution.py:302
  207.4 5.6 %collective-permute-start.21 = (bf16[64,512]{1,0:T(8,128)(2,1)}, bf16[64,512]{1,0:T(8,128)(2,1)S(1)}, u32[]{:S(2)}, u32[]{:S(2)}) collective-permute-start(bf16[64,512]{1,0:T(8,128)(2,1)} %finish.5), channel_id=1, source_target_pairs={{0,14},{1,15},{2,12},{3,13},{4,2},{5,3},{6,0},{7,1},{8,6},{9,7},{1... | collective-permute-start | bytes 196616 | tf_op jit(solution)/shard_map/ppermute | solution.py:302
  210.0 3.1 %copy-start.6 = (bf16[64,512]{1,0:T(8,128)(2,1)}, bf16[64,512]{1,0:T(8,128)(2,1)S(1)}, u32[]{:S(2)}) copy-start(bf16[64,512]{1,0:T(8,128)(2,1)S(1)} %collective-permute-done.18.refs_4_) | copy-start | bytes 196612
  211.2 1.9 copy-start.7
  212.9 0.6 copy-start.8
  213.6 0.6 copy-start.9
where the time goes:
time: 218 us
  Pallas kernels  144 us (66%)
  waiting for transfers between devices  30.6 us (14%)
  starting transfers between devices  28.2 us (13%)
  local copies, waits for them, and re-layouts  12.8 us (6%)
    pallas_call x6, Pallas kernels, project(): pl.pallas_call(functools.partial(project_kernel, tiles, ahead, len(pieces...  116 us
    ppermute x6, waiting for transfers between devices, onward(): lax.ppermute(piece, 'tensor', [(i, (i + 1) % n_tensor) for i in range(n_t...  16.5 us
    ppermute x7, starting transfers between devices, spread(): got.append(lax.ppermute(value, ('tensor', 'dp'), pairs))  13.1 us
    ppermute x9, waiting for transfers between devices, swap(): return lax.ppermute(value, axis, [(i, i ^ mask) for i in range(size)])  11 us
    slice x4, local copies, waits for them, and re-layouts, on_device(): cut = lambda source, offset, span: source[:, offset:offset + span]  10.8 us
    pallas_call x2, Pallas kernels, split_blocks(): pl.pallas_call(functools.partial(split_kernel, first), grid=(4,), in_spec...  10.7 us
    pallas_call x3, Pallas kernels, finish(): pl.pallas_call(finish_kernel, grid=(span // SMALL,), in_specs=[pl.BlockSp...  10.7 us
    ppermute x9, starting transfers between devices, swap(): return lax.ppermute(value, axis, [(i, i ^ mask) for i in range(size)])  9.73 us
  transfers between devices with their start and end apart: 22, of which 10 were waited for; matrix products, arithmetic and copies ran while one was open for 6% of the time, Pallas kernels for 63%

commit v1 on v0

--- a/solution.py
+++ b/solution.py
@@ -60,12 +60,13 @@
     gate_ref, proj_ref = take(2) if tiles else (None, None)
     (before_ref,) = take(1) if chained else (None,)
     (partial_ref,) = take(1) if carried else (None,)
-    sum_ref, odd_ref, even_ref = [refs.pop() for _ in range(3)] if tiles else (None,) * 3
+    sum_ref = refs.pop() if tiles else None
+    odd_ref, even_ref = [refs.pop() for _ in range(2)] if tiles and ahead else (None, None)
     later_ref = refs.pop() if ahead else None
     out_ref = refs.pop() if tiles else None
     step = pl.program_id(0)
 
-    def multiply(hidden_ref):
+    def product():
         hidden = partial_ref[...] if carried else None
         for k, grad_ref in enumerate(grads):
             for p in range(2):
@@ -73,7 +74,10 @@
                     weights[2 * k + p][...], grad_ref[p], preferred_element_type=jnp.float32
                 )
                 hidden = term if hidden is None else hidden + term
-        hidden_ref[...] = hidden
+        return hidden
+
+    def multiply(hidden_ref):
+        hidden_ref[...] = product()
 
     if not tiles:
         multiply(later_ref)
@@ -85,6 +89,18 @@
     @pl.when(step == 0)
     def _():
         sum_ref[...] = before_ref[...] if chained else jnp.zeros_like(sum_ref)
+
+    if not ahead:
+        sum_ref[...] += gated(product(), gate_ref, proj_ref)
+
+        @pl.when(step == tiles - 1)
+        def _():
+            out_ref[...] = sum_ref[...]
+
+        return
+
+    @pl.when(step == 0)
+    def _():
         odd_ref[...] = jnp.zeros_like(odd_ref)
 
     @pl.when((step < tiles) & (lax.rem(step, 2) == 0))
@@ -104,11 +120,9 @@
         reduce(even_ref if tiles % 2 else odd_ref)
         out_ref[...] = sum_ref[...]
 
-    if ahead:
-
-        @pl.when(step >= tiles)
-        def _():
-            multiply(later_ref)
+    @pl.when(step >= tiles)
+    def _():
+        multiply(later_ref)
 
 
 def project(shard, grads, gate, weights, proj, offset, span, extra, gate_column, before, partial, after):
@@ -121,7 +135,7 @@
     tiles, ahead = span // tile, extra // tile
     first, gate_first = offset // tile, gate_column // tile
     now = lambda i: jnp.minimum(i, tiles + ahead - 1)
-    last = lambda i: jnp.clip(i - 1, 0, max(tiles - 1, 0))
+    last = lambda i: jnp.clip(i - 1, 0, tiles - 1) if ahead else i
     chained, carried = before is not None, partial is not None
     total = pl.BlockSpec((k, rows), lambda i, s: (0, 0))
     later = pl.BlockSpec((tile, rows), lambda i, s: (jnp.maximum(i - tiles, 0), 0))
@@ -152,10 +166,11 @@
         functools.partial(project_kernel, tiles, ahead, len(pieces), chained, carried),
         grid_spec=pltpu.PrefetchScalarGridSpec(
             num_scalar_prefetch=1,
-            grid=(tiles + max(ahead, 1) if tiles else ahead,),
+            grid=(tiles + ahead,),
             in_specs=specs + [ANY] * len(after),
             out_specs=[total] * bool(tiles) + [later] * bool(ahead),
-            scratch_shapes=[hidden, hidden, pltpu.VMEM((k, rows), jnp.float32)] if tiles else [],
+            scratch_shapes=[hidden, hidden] * bool(tiles and ahead)
+            + [pltpu.VMEM((k, rows), jnp.float32)] * bool(tiles),
         ),
         out_shape=[jax.ShapeDtypeStruct((k, rows), jnp.float32)] * bool(tiles)
         + [jax.ShapeDtypeStruct((extra, rows), jnp.float32)] * bool(ahead),
@@ -320,7 +335,7 @@
     far_start = swap(far_blocks, "dp", n_dp, far)
     own = [own_blocks, onward(own_blocks)] if ring and n_tensor > 1 else [own_blocks]
     parts, _ = lax.optimization_barrier((parts, own[-1]))
-    far_gate, *last_gates = [swap(part, "dp", n_dp, far) for part in parts]
+    far_gate, *last_gates = [swap(part, "dp", n_dp, far) for part in parts[: len(parts) - bool(spans)]]
 
     def all_pairs(hold):
         blocks, _ = lax.optimization_barrier(((queries, far_query), hold))
@@ -333,10 +348,10 @@
         while len(own) <= split:
             own.append(onward(own[-1]))
         own_early = list(enumerate(own))[:split]
-        middle = hidden // (2 * TILE) * TILE if hidden % TILE == 0 else 0
-        halves = [(s, n) for s, n in ((0, middle), (middle, hidden - middle)) if n]
+        units = hidden // TILE if hidden % TILE == 0 else 0
+        halves = lambda cut: [(s, n) for s, n in ((0, cut * TILE), (cut * TILE, hidden - cut * TILE)) if n]
         own_sum, after = None, ()
-        for s, span in halves:
+        for s, span in halves(units // 3):
             (own_sum,) = project(
                 shard, own_early, gate_pre, weights, proj_out, s, span, 0, s, own_sum, None, after
             )
@@ -355,8 +370,8 @@
         while len(own) < n_tensor:
             own.append(onward(own[-1], first_sum))
         own_late = list(enumerate(own))[split:]
-        after = (partial,)
-        for s, span in halves:
+        after = (partial, pairs)
+        for s, span in halves(units // 2):
             (own_sum,) = project(
                 shard, own_late, gate_pre, weights, proj_out, s, span, 0, s, own_sum, None, after
             )
@@ -364,7 +379,7 @@
                 while len(others) < n_tensor:
                     hold = own_sum if len(others) == n_tensor - 1 else early_sum
                     others.append(onward(others[-1], hold))
-            after = (pairs, others[-2])
+            after = (others[-2],)
         far_late = list(enumerate(others))[split:]
     else:
         (own_sum,) = project(
@@ -378,8 +393,11 @@
     )
     both = jnp.concatenate([input_part, own_sum])
     both, far_gate = lax.optimization_barrier((both, far_gate))
-    terms = spread(both, 0)
-
+    terms = [lax.psum(both, "tensor")]
+
+    if spans:
+        final_gate, own_sum = lax.optimization_barrier((parts[-1], own_sum))
+        last_gates.append(swap(final_gate, "dp", n_dp, far))
     far_sum, *later = project(
         shard, far_late, far_gate, weights, proj_out, 0, main, sum(spans), 0, None, partial, (own_sum,)
     )
@@ -395,7 +413,7 @@
                 offsets[k],
                 far_sum,
                 jnp.bfloat16 if final else jnp.float32,
-                tuple(terms[1:]) if final else (),
+                (),
             )
     return score(terms, spread(far_sum, far), pairs)
 

time: 218 us -> 228 us (1.046)
  waiting for transfers between devices: 30.6 us -> 44.6 us
  between operations: 0.09 us -> 13.5 us
  starting transfers between devices: 28.2 us -> 17.3 us
  Pallas kernels: 144 us -> 135 us
    ppermute x6, waiting for transfers between devices: 16.5 us -> 25.6 us  [onward(): lax.ppermute(piece, 'tensor', [(i, (i + 1) % n_tensor) for i in range(n_t...]
    ppermute x7 -> x4, starting transfers between devices: 13.1 us -> 4.12 us  [spread(): got.append(lax.ppermute(value, ('tensor', 'dp'), pairs))]
    pallas_call x6, Pallas kernels: 116 us -> 108 us  [project(): pl.pallas_call(functools.partial(project_kernel, tiles, ahead, len(pieces...]
    ppermute x9, waiting for transfers between devices: 11 us -> 14 us  [swap(): return lax.ppermute(value, axis, [(i, i ^ mask) for i in range(size)])]
    ppermute x7 -> x4, waiting for transfers between devices: 3.11 us -> 4.94 us  [spread(): got.append(lax.ppermute(value, ('tensor', 'dp'), pairs))]
  transfers between devices with their start and end apart: 22 -> 20, of which waited for: 10 -> 13; matrix products, arithmetic and copies ran while one was open for 6% -> 6% of each run, Pallas kernels for 63% -> 58%
where the time goes in v1:
time: 228 us
  Pallas kernels  135 us (59%)
  waiting for transfers between devices  44.6 us (20%)
  starting transfers between devices  17.3 us (8%)
  local copies, waits for them, and re-layouts  14.7 us (6%)
  between operations  13.5 us (6%)
    pallas_call x6, Pallas kernels, project(): pl.pallas_call(functools.partial(project_kernel, tiles, ahead, len(pieces...  108 us
    ppermute x6, waiting for transfers between devices, onward(): lax.ppermute(piece, 'tensor', [(i, (i + 1) % n_tensor) for i in range(n_t...  25.6 us
    ppermute x9, waiting for transfers between devices, swap(): return lax.ppermute(value, axis, [(i, i ^ mask) for i in range(size)])  14 us
    pallas_call x2, Pallas kernels, split_blocks(): pl.pallas_call(functools.partial(split_kernel, first), grid=(4,), in_spec...  10.7 us
    pallas_call x3, Pallas kernels, finish(): pl.pallas_call(finish_kernel, grid=(span // SMALL,), in_specs=[pl.BlockSp...  10.7 us
    slice x4, local copies, waits for them, and re-layouts, on_device(): cut = lambda source, offset, span: source[:, offset:offset + span]  10.6 us
    ppermute x9, starting transfers between devices, swap(): return lax.ppermute(value, axis, [(i, i ^ mask) for i in range(size)])  9.7 us
    ppermute x4, waiting for transfers between devices, spread(): got.append(lax.ppermute(value, ('tensor', 'dp'), pairs))  4.94 us
  transfers between devices with their start and end apart: 20, of which 13 were waited for; matrix products, arithmetic and copies ran while one was open for 6% of the time, Pallas kernels for 58%

profile of v1, /device:TPU:0, one launch (start us, length us, event | category | flops | bytes accessed | tf_op | source)
XLA Modules:
  0.0 227.9 jit_solution(1373015368996652535)
XLA Ops:
  6.5 0.5 collective-permute-start.2
  7.0 1.3 slice.12.refs_0_
  8.3 2.8 %collective-permute-start.4 = (bf16[512,1024]{1,0:T(8,128)(2,1)S(1)}, bf16[512,1024]{1,0:T(8,128)(2,1)}, u32[]{:S(2)}, u32[]{:S(2)}) collective-permute-start(bf16[512,1024]{1,0:T(8,128)(2,1)S(1)} %slice.12.refs_0_), channel_id=1, source_target_pairs={{0,2},{1,3},{2,0},{3,1},{4,6},{5,7},{6,4},{7,5},{8,10},{9,11},{10,... | collective-permute-start | bytes 3145736 | tf_op jit(solution)/shard_map/ppermute | solution.py:18
  11.1 5.4 %split_blocks.2.refs_0_ = bf16[2,512,512]{2,1,0:T(8,128)(2,1)} custom-call(bf16[512,4,512]{2,1,0:T(4,128)(2,1)} %grad_ref.3, bf16[512,1024]{1,0:T(8,128)(2,1)} %copy-done.3), custom_call_target="tpu_custom_call" | custom-call | tf_op jit(solution)/shard_map/split_blocks/pallas_call | solution.py:37
  16.4 1.6 collective-permute-start
  18.0 0.9 collective-permute-start.5
  18.9 5.3 %split_blocks.3 = bf16[2,512,512]{2,1,0:T(8,128)(2,1)} custom-call(bf16[512,4,512]{2,1,0:T(4,128)(2,1)} %grad_ref.3, bf16[2,512,512]{2,1,0:T(8,128)(2,1)} %split_blocks.2.refs_0_), custom_call_target="tpu_custom_call" | custom-call | tf_op jit(solution)/shard_map/split_blocks/pallas_call | solution.py:37
  24.2 1.9 slice.15
  26.1 2.7 %slice.14 = bf16[512,1536]{1,0:T(8,128)(2,1)} slice(bf16[512,7168]{1,0:T(8,128)(2,1)} %refs_6_.7), slice={[0:512], [4096:5632]} | slice | bytes 3145728 | tf_op jit(solution)/shard_map/slice | solution.py:322
  28.8 4.8 %slice.13 = bf16[512,4096]{1,0:T(8,128)(2,1)} slice(bf16[512,7168]{1,0:T(8,128)(2,1)} %refs_6_.7), slice={[0:512], [0:4096]} | slice | bytes 8388608 | tf_op jit(solution)/shard_map/slice | solution.py:322
  33.5 4.0 %collective-permute-done.5.refs_1_ = bf16[64,1024]{1,0:T(8,128)(2,1)S(1)} collective-permute-done((bf16[64,1024]{1,0:T(8,128)(2,1)S(1)}, bf16[64,1024]{1,0:T(8,128)(2,1)S(1)}, u32[]{:S(2)}, u32[]{:S(2)}) %collective-permute-start.5) | collective-permute-done | bytes 131104 | tf_op jit(solution)/shard_map/ppermute | solution.py:18
  37.5 0.0 collective-permute-done.4.gate_ref
  37.5 1.7 collective-permute-start.6
  39.3 4.4 %collective-permute-done.refs_1_ = bf16[2,512,512]{2,1,0:T(8,128)(2,1)} collective-permute-done((bf16[2,512,512]{2,1,0:T(8,128)(2,1)}, bf16[2,512,512]{2,1,0:T(8,128)(2,1)}, u32[]{:S(2)}, u32[]{:S(2)}) %collective-permute-start) | collective-permute-done | bytes 1048608 | tf_op jit(solution)/shard_map/ppermute | solution.py:300
  43.7 0.0 collective-permute-start.1
  43.7 1.2 collective-permute-start.11
  44.9 5.2 %collective-permute-done.2.refs_3_.refs_5_ = bf16[7168,2048]{1,0:T(8,128)(2,1)} collective-permute-done((bf16[7168,2048]{1,0:T(8,128)(2,1)}, bf16[7168,2048]{1,0:T(8,128)(2,1)}, u32[]{:S(2)}, u32[]{:S(2)}) %collective-permute-start.2) | collective-permute-done | bytes 29360160 | tf_op jit(solution)/shard_map/ppermute | solution.py:18
  50.1 10.0 %project.6.refs_8_ = f32[64,512]{1,0:T(8,128)} custom-call(s32[1]{0:T(128)} %bitcast.shard_ref, bf16[2,512,512]{2,1,0:T(8,128)(2,1)} %split_blocks.2.refs_0_, bf16[2,512,512]{2,1,0:T(8,128)(2,1)} %collective-permute-done.refs_1_, bf16[7168,2048]{1,0:T(8,128)(2,1)} %refs_4_.11, bf16[7168,2048]{1,0:T(8,128)(2,1)} %collective-permute-done.2.refs_3_.refs_5_, ...), custom_call_target="tpu_custom_call" | custom-call | flops 4294967296 | bytes 10485760 | tf_op jit(solution)/shard_map/project/pallas_call | solution.py:165
  60.1 3.7 %collective-permute-done.6.refs_0_ = bf16[2,512,512]{2,1,0:T(8,128)(2,1)} collective-permute-done((bf16[2,512,512]{2,1,0:T(8,128)(2,1)}, bf16[2,512,512]{2,1,0:T(8,128)(2,1)}, u32[]{:S(2)}, u32[]{:S(2)}) %collective-permute-start.6) | collective-permute-done | bytes 1048608 | tf_op jit(solution)/shard_map/ppermute | solution.py:18
  63.9 1.9 collective-permute-start.7
  65.7 6.1 %collective-permute-done.1.refs_9_.refs_0_ = bf16[2,512,512]{2,1,0:T(8,128)(2,1)S(1)} collective-permute-done((bf16[2,512,512]{2,1,0:T(8,128)(2,1)}, bf16[2,512,512]{2,1,0:T(8,128)(2,1)S(1)}, u32[]{:S(2)}, u32[]{:S(2)}) %collective-permute-start.1) | collective-permute-done | bytes 1048608 | tf_op jit(solution)/shard_map/ppermute | solution.py:300
  71.8 1.0 copy-done.1
  72.8 18.5 %project.7.refs_6_.refs_8_ = f32[64,512]{1,0:T(8,128)} custom-call(s32[1]{0:T(128)} %bitcast.shard_ref, bf16[2,512,512]{2,1,0:T(8,128)(2,1)} %split_blocks.2.refs_0_, bf16[2,512,512]{2,1,0:T(8,128)(2,1)} %collective-permute-done.refs_1_, bf16[7168,2048]{1,0:T(8,128)(2,1)} %refs_4_.11, bf16[7168,2048]{1,0:T(8,128)(2,1)} %collective-permute-done.2.refs_3_.refs_5_, ...), custom_call_target="tpu_custom_call" | custom-call | flops 10737418240 | bytes 26214400 | tf_op jit(solution)/shard_map/project/pallas_call | solution.py:165
  91.2 0.0 collective-permute-start.8
  91.2 0.5 collective-permute-start.9
  91.7 0.0 collective-permute-start.3
  91.7 0.8 collective-permute-done.8.refs_2_
  92.6 0.2 collective-permute-done.9.refs_3_
  92.8 0.5 copy-done.8
  93.2 0.7 copy-done.9
  93.9 2.4 %pair_queries.1.refs_10_.refs_5_ = bf16[4096,128]{1,0:T(8,128)(2,1)} custom-call(bf16[64,1024]{1,0:T(8,128)(2,1)} %refs_0_, bf16[64,1024]{1,0:T(8,128)(2,1)} %copy-done.7, bf16[64,1024]{1,0:T(8,128)(2,1)} %copy-done.8, bf16[64,1024]{1,0:T(8,128)(2,1)} %copy-done.9), custom_call_target="tpu_custom_call" | custom-call | tf_op jit(solution)/shard_map/pair_queries/pallas_call | solution.py:262
  96.3 0.0 collective-permute-done.7.refs_1_
  96.3 0.0 collective-permute-start.10
  96.3 22.9 %project.8.refs_9_.refs_8_ = f32[7168,512]{1,0:T(8,128)} custom-call(s32[1]{0:T(128)} %bitcast.shard_ref, bf16[2,512,512]{2,1,0:T(8,128)(2,1)} %collective-permute-done.6.refs_0_, bf16[2,512,512]{2,1,0:T(8,128)(2,1)} %collective-permute-done.7.refs_1_, bf16[7168,2048]{1,0:T(8,128)(2,1)} %refs_4_.11, ...), custom_call_target="tpu_custom_call" | custom-call | flops 15032385536 | bytes 36700160 | tf_op jit(solution)/shard_map/project/pallas_call | solution.py:165
  119.2 0.7 collective-permute-done.3.refs_1_
  119.9 13.0 %project.9.refs_8_ = f32[64,512]{1,0:T(8,128)} custom-call(s32[1]{0:T(128)} %bitcast.shard_ref, bf16[2,512,512]{2,1,0:T(8,128)(2,1)} %copy-done.1, bf16[2,512,512]{2,1,0:T(8,128)(2,1)} %collective-permute-done.3.refs_1_, bf16[7168,2048]{1,0:T(8,128)(2,1)} %refs_4_.11, bf16[7168,2048]{1,0:T(8,128)(2,1)} %collective-permute-done.2.refs_3_.refs_5_, ...), custom_call_target="tpu_custom_call" | custom-call | flops 6442450944 | bytes 15728640 | tf_op jit(solution)/shard_map/project/pallas_call | solution.py:165
  132.8 8.5 %collective-permute-done.10.refs_9_.refs_0_ = bf16[2,512,512]{2,1,0:T(8,128)(2,1)S(1)} collective-permute-done((bf16[2,512,512]{2,1,0:T(8,128)(2,1)}, bf16[2,512,512]{2,1,0:T(8,128)(2,1)S(1)}, u32[]{:S(2)}, u32[]{:S(2)}) %collective-permute-start.10) | collective-permute-done | bytes 1048608 | tf_op jit(solution)/shard_map/ppermute | solution.py:300
  141.4 0.0 collective-permute-start.12
  141.4 0.8 fusion
  142.1 1.3 collective-permute-start.14
  143.4 15.7 %project.10.refs_9_ = f32[64,512]{1,0:T(8,128)} custom-call(s32[1]{0:T(128)} %bitcast.shard_ref, bf16[2,512,512]{2,1,0:T(8,128)(2,1)} %copy-done.1, bf16[2,512,512]{2,1,0:T(8,128)(2,1)} %collective-permute-done.3.refs_1_, bf16[7168,2048]{1,0:T(8,128)(2,1)} %refs_4_.11, bf16[7168,2048]{1,0:T(8,128)(2,1)} %collective-permute-done.2.refs_3_.refs_5_, ...), custom_call_target="tpu_custom_call" | custom-call | flops 8589934592 | bytes 20971520 | tf_op jit(solution)/shard_map/project/pallas_call | solution.py:165
  159.1 1.6 pad_maximum_fusion
  160.7 0.0 collective-permute-done.11.refs_6_
  160.7 0.0 all-reduce.2.cloned.1.call-update
  160.8 0.9 collective-permute-start.13
  161.7 5.9 %collective-permute-done.12.refs_1_ = bf16[2,512,512]{2,1,0:T(8,128)(2,1)} collective-permute-done((bf16[2,512,512]{2,1,0:T(8,128)(2,1)S(1)}, bf16[2,512,512]{2,1,0:T(8,128)(2,1)}, u32[]{:S(2)}, u32[]{:S(2)}) %collective-permute-start.12) | collective-permute-done | bytes 1048608 | tf_op jit(solution)/shard_map/ppermute | solution.py:300
  167.6 28.3 %project.11 = (f32[64,512]{1,0:T(8,128)}, f32[3072,512]{1,0:T(8,128)}) custom-call(s32[1]{0:T(128)} %bitcast.shard_ref, bf16[2,512,512]{2,1,0:T(8,128)(2,1)} %copy-done.2, bf16[2,512,512]{2,1,0:T(8,128)(2,1)} %collective-permute-done.12.refs_1_, bf16[7168,2048]{1,0:T(8,128)(2,1)} %refs_4_.11, bf16[7168,2048]{1,0:T(8,128)(2,1)} %collective-permute-done.2.refs_3_.refs_5_, ...), custom_call_target="tpu_custom_call" | custom-call | flops 15032385536 | bytes 36700160 | tf_op jit(solution)/shard_map/project/pallas_call | solution.py:165
  195.8 3.2 %finish.3.before_ref = f32[64,512]{1,0:T(8,128)} custom-call(f32[3072,512]{1,0:T(8,128)} %get-tuple-element.42.hidden_ref, bf16[512,1024]{1,0:T(8,128)(2,1)} %collective-permute-done.4.gate_ref, bf16[64,7168]{1,0:T(8,128)(2,1)} %bitcast.9, f32[64,512]{1,0:T(8,128)} %get-tuple-element.46.before_ref), custom_call_target="tpu_custom_call" | custom-call | tf_op jit(solution)/shard_map/finish/pallas_call | solution.py:209
  199.1 0.0 collective-permute-done.14.gate_ref
  199.1 4.9 %finish.4.before_ref = f32[64,512]{1,0:T(8,128)} custom-call(f32[3072,512]{1,0:T(8,128)} %get-tuple-element.42.hidden_ref, bf16[512,1536]{1,0:T(8,128)(2,1)} %collective-permute-done.14.gate_ref, bf16[64,7168]{1,0:T(8,128)(2,1)} %bitcast.10, f32[64,512]{1,0:T(8,128)} %finish.3.before_ref), custom_call_target="tpu_custom_call" | custom-call | tf_op jit(solution)/shard_map/finish/pallas_call | solution.py:209
  204.0 0.0 collective-permute-done.13.gate_ref
  204.0 0.8 copy-done.4
  204.8 2.5 %finish.5 = bf16[64,512]{1,0:T(8,128)(2,1)} custom-call(f32[3072,512]{1,0:T(8,128)} %get-tuple-element.42.hidden_ref, bf16[512,512]{1,0:T(8,128)(2,1)} %copy-done.4, bf16[64,7168]{1,0:T(8,128)(2,1)} %bitcast.11, f32[64,512]{1,0:T(8,128)} %finish.4.before_ref), custom_call_target="tpu_custom_call" | custom-call | tf_op jit(solution)/shard_map/finish/pallas_call | solution.py:209
  207.3 0.2 collective-permute-start.18
  207.5 0.7 collective-permute-start.17
  208.2 2.0 collective-permute-start.16
  210.2 1.2 collective-permute-start.15
  211.4 1.2 collective-permute-done.18.refs_4_
  212.7 1.5 collective-permute-done.17.refs_3_
  214.2 2.2 collective-permute-done.16.refs_2_
  216.4 0.0 collective-permute-done.15.refs_1_
  216.4 0.6 copy-done.12
  217.0 0.6 copy-done.13
  217.6 3.4 %score.1 = f32[64,512]{1,0:T(8,128)} custom-call(f32[128,512]{1,0:T(8,128)} %all-reduce.2.cloned.1.call-done.refs_0_, bf16[64,512]{1,0:T(8,128)(2,1)} %copy-done.13, bf16[64,512]{1,0:T(8,128)(2,1)} %copy-done.12, bf16[64,512]{1,0:T(8,128)(2,1)} %copy-done.11, bf16[64,512]{1,0:T(8,128)(2,1)} %copy-done.10, bf16[4096,128]{1,0:T(8,128)(2,1)} %pair_queries.1.refs_10_.refs_5_), custom_call_target="tpu_custom_call" | custom-call | tf_op jit(solution)/shard_map/score/pallas_call | solution.py:272
  (24 shorter events, 0.0 us)
Async XLA Ops:
  6.5 134.8 %copy-start = (bf16[512,2048]{1,0:T(8,128)(2,1)S(1)}, bf16[512,2048]{1,0:T(8,128)(2,1)}, u32[]{:S(2)}) copy-start(bf16[512,2048]{1,0:T(8,128)(2,1)} %param.7) | copy-start | bytes 6291460
  6.5 11.5 %copy-start.6 = (bf16[64,1024]{1,0:T(8,128)(2,1)S(1)}, bf16[64,1024]{1,0:T(8,128)(2,1)}, u32[]{:S(2)}) copy-start(bf16[64,1024]{1,0:T(8,128)(2,1)} %refs_0_) | copy-start | bytes 393220
  6.5 204.9 %all-reduce.2.cloned.1.call-start = ((), (), s32[]{:S(2)}) async-start(), calls=%async_computation | async-start | bytes 524288 | tf_op jit(solution)/shard_map/psum | solution.py:396
  6.5 43.6 %collective-permute-start.2 = (bf16[7168,2048]{1,0:T(8,128)(2,1)}, bf16[7168,2048]{1,0:T(8,128)(2,1)}, u32[]{:S(2)}, u32[]{:S(2)}) collective-permute-start(bf16[7168,2048]{1,0:T(8,128)(2,1)} %refs_4_.11), channel_id=1, source_target_pairs={{0,1},{1,0},{2,3},{3,2},{4,5},{5,4},{6,7},{7,6},{8,9},{9,8},{10,11... | collective-permute-start | bytes 88080392 | tf_op jit(solution)/shard_map/ppermute | solution.py:18
  8.3 2.8 %copy-start.3 = (bf16[512,1024]{1,0:T(8,128)(2,1)}, bf16[512,1024]{1,0:T(8,128)(2,1)S(1)}, u32[]{:S(2)}) copy-start(bf16[512,1024]{1,0:T(8,128)(2,1)S(1)} %slice.12.refs_0_) | copy-start | bytes 3145732
  8.3 29.2 %collective-permute-start.4 = (bf16[512,1024]{1,0:T(8,128)(2,1)S(1)}, bf16[512,1024]{1,0:T(8,128)(2,1)}, u32[]{:S(2)}, u32[]{:S(2)}) collective-permute-start(bf16[512,1024]{1,0:T(8,128)(2,1)S(1)} %slice.12.refs_0_), channel_id=1, source_target_pairs={{0,2},{1,3},{2,0},{3,1},{4,6},{5,7},{6,4},{7,5},{8,10},{9,11},{10,... | collective-permute-start | bytes 3145736 | tf_op jit(solution)/shard_map/ppermute | solution.py:18
  16.4 27.3 %collective-permute-start = (bf16[2,512,512]{2,1,0:T(8,128)(2,1)}, bf16[2,512,512]{2,1,0:T(8,128)(2,1)}, u32[]{:S(2)}, u32[]{:S(2)}) collective-permute-start(bf16[2,512,512]{2,1,0:T(8,128)(2,1)} %split_blocks.2.refs_0_), channel_id=1, source_target_pairs={{0,4},{4,8},{8,12},{12,0},{1,5},{5,9},{9,13},{13,1},{2,6},{6,10},{... | collective-permute-start | bytes 3145736 | tf_op jit(solution)/shard_map/ppermute | solution.py:300
  18.0 19.5 %collective-permute-start.5 = (bf16[64,1024]{1,0:T(8,128)(2,1)S(1)}, bf16[64,1024]{1,0:T(8,128)(2,1)S(1)}, u32[]{:S(2)}, u32[]{:S(2)}) collective-permute-start(bf16[64,1024]{1,0:T(8,128)(2,1)S(1)} %copy-done.6), channel_id=1, source_target_pairs={{0,2},{1,3},{2,0},{3,1},{4,6},{5,7},{6,4},{7,5},{8,10},{9,11},{10,... | collective-permute-start | bytes 393224 | tf_op jit(solution)/shard_map/ppermute | solution.py:18
  37.5 53.7 %copy-start.7 = (bf16[64,1024]{1,0:T(8,128)(2,1)}, bf16[64,1024]{1,0:T(8,128)(2,1)S(1)}, u32[]{:S(2)}) copy-start(bf16[64,1024]{1,0:T(8,128)(2,1)S(1)} %collective-permute-done.5.refs_1_) | copy-start | bytes 393220
  37.5 26.3 %collective-permute-start.6 = (bf16[2,512,512]{2,1,0:T(8,128)(2,1)}, bf16[2,512,512]{2,1,0:T(8,128)(2,1)}, u32[]{:S(2)}, u32[]{:S(2)}) collective-permute-start(bf16[2,512,512]{2,1,0:T(8,128)(2,1)} %split_blocks.3), channel_id=1, source_target_pairs={{0,2},{1,3},{2,0},{3,1},{4,6},{5,7},{6,4},{7,5},{8,10},{9,11},{10,... | collective-permute-start | bytes 3145736 | tf_op jit(solution)/shard_map/ppermute | solution.py:18
  43.7 28.1 %collective-permute-start.1 = (bf16[2,512,512]{2,1,0:T(8,128)(2,1)}, bf16[2,512,512]{2,1,0:T(8,128)(2,1)S(1)}, u32[]{:S(2)}, u32[]{:S(2)}) collective-permute-start(bf16[2,512,512]{2,1,0:T(8,128)(2,1)} %collective-permute-done.refs_1_), channel_id=1, source_target_pairs={{0,4},{4,8},{8,12},{12,0},{1,5},{5,9},{9,13},{13,1},{2,6},{6,10},{... | collective-permute-start | bytes 3145736 | tf_op jit(solution)/shard_map/ppermute | solution.py:300
  43.7 117.0 %collective-permute-start.11 = (bf16[512,4096]{1,0:T(8,128)(2,1)}, bf16[512,4096]{1,0:T(8,128)(2,1)}, u32[]{:S(2)}, u32[]{:S(2)}) collective-permute-start(bf16[512,4096]{1,0:T(8,128)(2,1)} %slice.13), channel_id=1, source_target_pairs={{0,2},{1,3},{2,0},{3,1},{4,6},{5,7},{6,4},{7,5},{8,10},{9,11},{10,... | collective-permute-start | bytes 12582920 | tf_op jit(solution)/shard_map/ppermute | solution.py:18
  63.9 32.4 %collective-permute-start.7 = (bf16[2,512,512]{2,1,0:T(8,128)(2,1)}, bf16[2,512,512]{2,1,0:T(8,128)(2,1)}, u32[]{:S(2)}, u32[]{:S(2)}) collective-permute-start(bf16[2,512,512]{2,1,0:T(8,128)(2,1)} %collective-permute-done.6.refs_0_), channel_id=1, source_target_pairs={{0,4},{4,8},{8,12},{12,0},{1,5},{5,9},{9,13},{13,1},{2,6},{6,10},{... | collective-permute-start | bytes 3145736 | tf_op jit(solution)/shard_map/ppermute | solution.py:300
  71.8 1.0 copy-start.1
  91.2 1.3 collective-permute-start.8
  91.2 1.5 collective-permute-start.9
  91.7 28.1 %collective-permute-start.3 = (bf16[2,512,512]{2,1,0:T(8,128)(2,1)}, bf16[2,512,512]{2,1,0:T(8,128)(2,1)}, u32[]{:S(2)}, u32[]{:S(2)}) collective-permute-start(bf16[2,512,512]{2,1,0:T(8,128)(2,1)} %copy-done.1), channel_id=1, source_target_pairs={{0,4},{4,8},{8,12},{12,0},{1,5},{5,9},{9,13},{13,1},{2,6},{6,10},{... | collective-permute-start | bytes 3145736 | tf_op jit(solution)/shard_map/ppermute | solution.py:300
  92.6 0.7 copy-start.8
  93.2 0.7 copy-start.9
  96.3 45.1 %collective-permute-start.10 = (bf16[2,512,512]{2,1,0:T(8,128)(2,1)}, bf16[2,512,512]{2,1,0:T(8,128)(2,1)S(1)}, u32[]{:S(2)}, u32[]{:S(2)}) collective-permute-start(bf16[2,512,512]{2,1,0:T(8,128)(2,1)} %collective-permute-done.7.refs_1_), channel_id=1, source_target_pairs={{0,4},{4,8},{8,12},{12,0},{1,5},{5,9},{9,13},{13,1},{2,6},{6,10},{... | collective-permute-start | bytes 3145736 | tf_op jit(solution)/shard_map/ppermute | solution.py:300
  119.2 22.2 %copy-start.5 = (bf16[2048,64]{0,1:T(8,128)(2,1)S(1)}, bf16[2048,64]{0,1:T(8,128)(2,1)}, u32[]{:S(2)}) copy-start(bf16[2048,64]{0,1:T(8,128)(2,1)} %param.11) | copy-start | bytes 786436
  141.4 2.0 copy-start.2
  141.4 26.2 %collective-permute-start.12 = (bf16[2,512,512]{2,1,0:T(8,128)(2,1)S(1)}, bf16[2,512,512]{2,1,0:T(8,128)(2,1)}, u32[]{:S(2)}, u32[]{:S(2)}) collective-permute-start(bf16[2,512,512]{2,1,0:T(8,128)(2,1)S(1)} %collective-permute-done.10.refs_9_.refs_0_), channel_id=1, source_target_pairs={{0,4},{4,8},{8,12},{12,0},{1,5},{5,9},{9,13},{13,1},{2,6},{6,10},{... | collective-permute-start | bytes 3145736 | tf_op jit(solution)/shard_map/ppermute | solution.py:300
  142.1 56.9 %collective-permute-start.14 = (bf16[512,1536]{1,0:T(8,128)(2,1)}, bf16[512,1536]{1,0:T(8,128)(2,1)}, u32[]{:S(2)}, u32[]{:S(2)}) collective-permute-start(bf16[512,1536]{1,0:T(8,128)(2,1)} %slice.14), channel_id=1, source_target_pairs={{0,2},{1,3},{2,0},{3,1},{4,6},{5,7},{6,4},{7,5},{8,10},{9,11},{10,... | collective-permute-start | bytes 4718600 | tf_op jit(solution)/shard_map/ppermute | solution.py:18
  160.8 43.2 %collective-permute-start.13 = (bf16[512,512]{1,0:T(8,128)(2,1)}, bf16[512,512]{1,0:T(8,128)(2,1)S(1)}, u32[]{:S(2)}, u32[]{:S(2)}) collective-permute-start(bf16[512,512]{1,0:T(8,128)(2,1)} %slice.15), channel_id=1, source_target_pairs={{0,2},{1,3},{2,0},{3,1},{4,6},{5,7},{6,4},{7,5},{8,10},{9,11},{10,... | collective-permute-start | bytes 1572872 | tf_op jit(solution)/shard_map/ppermute | solution.py:18
  204.0 0.8 copy-start.4
  207.3 5.4 %collective-permute-start.18 = (bf16[64,512]{1,0:T(8,128)(2,1)}, bf16[64,512]{1,0:T(8,128)(2,1)S(1)}, u32[]{:S(2)}, u32[]{:S(2)}) collective-permute-start(bf16[64,512]{1,0:T(8,128)(2,1)} %finish.5), channel_id=1, source_target_pairs={{0,14},{1,15},{2,12},{3,13},{4,2},{5,3},{6,0},{7,1},{8,6},{9,7},{1... | collective-permute-start | bytes 196616 | tf_op jit(solution)/shard_map/ppermute | solution.py:317
  207.5 6.7 %collective-permute-start.17 = (bf16[64,512]{1,0:T(8,128)(2,1)}, bf16[64,512]{1,0:T(8,128)(2,1)S(1)}, u32[]{:S(2)}, u32[]{:S(2)}) collective-permute-start(bf16[64,512]{1,0:T(8,128)(2,1)} %finish.5), channel_id=1, source_target_pairs={{0,10},{1,11},{2,8},{3,9},{4,14},{5,15},{6,12},{7,13},{8,2},{9,3},... | collective-permute-start | bytes 196616 | tf_op jit(solution)/shard_map/ppermute | solution.py:317
  208.2 8.2 %collective-permute-start.16 = (bf16[64,512]{1,0:T(8,128)(2,1)}, bf16[64,512]{1,0:T(8,128)(2,1)S(1)}, u32[]{:S(2)}, u32[]{:S(2)}) collective-permute-start(bf16[64,512]{1,0:T(8,128)(2,1)} %finish.5), channel_id=1, source_target_pairs={{0,6},{1,7},{2,4},{3,5},{4,10},{5,11},{6,8},{7,9},{8,14},{9,15},{1... | collective-permute-start | bytes 196616 | tf_op jit(solution)/shard_map/ppermute | solution.py:317
  210.2 6.1 %collective-permute-start.15 = (bf16[64,512]{1,0:T(8,128)(2,1)}, bf16[64,512]{1,0:T(8,128)(2,1)S(1)}, u32[]{:S(2)}, u32[]{:S(2)}) collective-permute-start(bf16[64,512]{1,0:T(8,128)(2,1)} %finish.5), channel_id=1, source_target_pairs={{0,2},{1,3},{2,0},{3,1},{4,6},{5,7},{6,4},{7,5},{8,10},{9,11},{10,... | collective-permute-start | bytes 196616 | tf_op jit(solution)/shard_map/ppermute | solution.py:317
  212.7 3.7 %copy-start.10 = (bf16[64,512]{1,0:T(8,128)(2,1)}, bf16[64,512]{1,0:T(8,128)(2,1)S(1)}, u32[]{:S(2)}) copy-start(bf16[64,512]{1,0:T(8,128)(2,1)S(1)} %collective-permute-done.18.refs_4_) | copy-start | bytes 196612
  214.2 2.2 copy-start.11
  216.4 0.6 copy-start.12
  217.0 0.6 copy-start.13
Sparse Core Ops, SparseCore 0:
  160.9 36.1 all-reduce.1

commit v2 on v1

--- a/solution.py
+++ b/solution.py
@@ -359,7 +359,7 @@
                 first_sum = own_sum
             after = (own[-1],)
         early_sum = own_sum
-        pairs = all_pairs(early_sum)
+        pairs = all_pairs(own[1])
         others = [far_start]
         for _ in range(split - 1):
             others.append(onward(others[-1], first_sum))
@@ -393,7 +393,7 @@
     )
     both = jnp.concatenate([input_part, own_sum])
     both, far_gate = lax.optimization_barrier((both, far_gate))
-    terms = [lax.psum(both, "tensor")]
+    terms = spread(both, 0)
 
     if spans:
         final_gate, own_sum = lax.optimization_barrier((parts[-1], own_sum))

time: 228 us -> 214 us (0.939)
  between operations: 13.5 us -> 0.11 us
  starting transfers between devices: 17.3 us -> 24.8 us
  waiting for transfers between devices: 44.6 us -> 37.6 us
    ppermute x4 -> x7, starting transfers between devices: 4.12 us -> 10.8 us  [spread(): got.append(lax.ppermute(value, ('tensor', 'dp'), pairs))]
    ppermute x6, waiting for transfers between devices: 25.6 us -> 19.5 us  [onward(): lax.ppermute(piece, 'tensor', [(i, (i + 1) % n_tensor) for i in range(n_t...]
    ppermute x4 -> x7, waiting for transfers between devices: 4.94 us -> 3.93 us  [spread(): got.append(lax.ppermute(value, ('tensor', 'dp'), pairs))]
  transfers between devices with their start and end apart: 20 -> 22, of which waited for: 13 -> 11; matrix products, arithmetic and copies ran while one was open for 6% -> 6% of each run, Pallas kernels for 58% -> 62%
where the time goes in v2:
time: 214 us; the launch traced here: 213 us
  Pallas kernels  136 us (64%)
  waiting for transfers between devices  37.6 us (18%)
  starting transfers between devices  24.8 us (12%)
  local copies, waits for them, and re-layouts  13.5 us (6%)
    pallas_call x6, Pallas kernels, project(): pl.pallas_call(functools.partial(project_kernel, tiles, ahead, len(pieces...  108 us
    ppermute x6, waiting for transfers between devices, onward(): lax.ppermute(piece, 'tensor', [(i, (i + 1) % n_tensor) for i in range(n_t...  19.5 us
    ppermute x9, waiting for transfers between devices, swap(): return lax.ppermute(value, axis, [(i, i ^ mask) for i in range(size)])  14.1 us
    ppermute x9, starting transfers between devices, swap(): return lax.ppermute(value, axis, [(i, i ^ mask) for i in range(size)])  10.9 us
    ppermute x7, starting transfers between devices, spread(): got.append(lax.ppermute(value, ('tensor', 'dp'), pairs))  10.8 us
    pallas_call x2, Pallas kernels, split_blocks(): pl.pallas_call(functools.partial(split_kernel, first), grid=(4,), in_spec...  10.7 us
    pallas_call x3, Pallas kernels, finish(): pl.pallas_call(finish_kernel, grid=(span // SMALL,), in_specs=[pl.BlockSp...  10.7 us
    slice x4, local copies, waits for them, and re-layouts, on_device(): cut = lambda source, offset, span: source[:, offset:offset + span]  10.6 us
  transfers between devices with their start and end apart: 22, of which 11 were waited for; matrix products, arithmetic and copies ran while one was open for 6% of the time, Pallas kernels for 62%

profile of v2, /device:TPU:0, one launch (start us, length us, event | category | flops | bytes accessed | tf_op | source)
XLA Modules:
  0.0 213.4 jit_solution(1765632250870018126)
XLA Ops:
  0.0 0.5 collective-permute-start.2
  0.5 1.3 slice.12.refs_0_
  1.8 2.7 %collective-permute-start.4 = (bf16[512,1024]{1,0:T(8,128)(2,1)S(1)}, bf16[512,1024]{1,0:T(8,128)(2,1)}, u32[]{:S(2)}, u32[]{:S(2)}) collective-permute-start(bf16[512,1024]{1,0:T(8,128)(2,1)S(1)} %slice.12.refs_0_), channel_id=1, source_target_pairs={{0,2},{1,3},{2,0},{3,1},{4,6},{5,7},{6,4},{7,5},{8,10},{9,11},{10,... | collective-permute-start | bytes 3145736 | tf_op jit(solution)/shard_map/ppermute | solution.py:18
  4.5 5.4 %split_blocks.2.refs_0_ = bf16[2,512,512]{2,1,0:T(8,128)(2,1)} custom-call(bf16[512,4,512]{2,1,0:T(4,128)(2,1)} %grad_ref.3, bf16[512,1024]{1,0:T(8,128)(2,1)} %copy-done.2), custom_call_target="tpu_custom_call" | custom-call | tf_op jit(solution)/shard_map/split_blocks/pallas_call | solution.py:37
  9.9 1.6 collective-permute-start
  11.5 0.9 collective-permute-start.5
  12.4 4.7 %slice.13 = bf16[512,4096]{1,0:T(8,128)(2,1)} slice(bf16[512,7168]{1,0:T(8,128)(2,1)} %refs_6_.7), slice={[0:512], [0:4096]} | slice | bytes 8388608 | tf_op jit(solution)/shard_map/slice | solution.py:322
  17.1 2.7 %slice.14 = bf16[512,1536]{1,0:T(8,128)(2,1)} slice(bf16[512,7168]{1,0:T(8,128)(2,1)} %refs_6_.7), slice={[0:512], [4096:5632]} | slice | bytes 3145728 | tf_op jit(solution)/shard_map/slice | solution.py:322
  19.8 1.9 slice.15
  21.7 5.3 %split_blocks.3 = bf16[2,512,512]{2,1,0:T(8,128)(2,1)} custom-call(bf16[512,4,512]{2,1,0:T(4,128)(2,1)} %grad_ref.3, bf16[2,512,512]{2,1,0:T(8,128)(2,1)} %split_blocks.2.refs_0_), custom_call_target="tpu_custom_call" | custom-call | tf_op jit(solution)/shard_map/split_blocks/pallas_call | solution.py:37
  27.0 3.9 %collective-permute-done.5.refs_1_ = bf16[64,1024]{1,0:T(8,128)(2,1)S(1)} collective-permute-done((bf16[64,1024]{1,0:T(8,128)(2,1)S(1)}, bf16[64,1024]{1,0:T(8,128)(2,1)S(1)}, u32[]{:S(2)}, u32[]{:S(2)}) %collective-permute-start.5) | collective-permute-done | bytes 131104 | tf_op jit(solution)/shard_map/ppermute | solution.py:18
  31.0 0.0 collective-permute-done.4.gate_ref
  31.0 1.7 collective-permute-start.6
  32.7 4.5 %collective-permute-done.refs_1_ = bf16[2,512,512]{2,1,0:T(8,128)(2,1)} collective-permute-done((bf16[2,512,512]{2,1,0:T(8,128)(2,1)}, bf16[2,512,512]{2,1,0:T(8,128)(2,1)}, u32[]{:S(2)}, u32[]{:S(2)}) %collective-permute-start) | collective-permute-done | bytes 1048608 | tf_op jit(solution)/shard_map/ppermute | solution.py:300
  37.2 0.0 collective-permute-start.1
  37.2 0.0 collective-permute-start.8
  37.2 0.5 collective-permute-start.9
  37.7 5.9 %collective-permute-done.2.refs_3_.refs_5_ = bf16[7168,2048]{1,0:T(8,128)(2,1)} collective-permute-done((bf16[7168,2048]{1,0:T(8,128)(2,1)}, bf16[7168,2048]{1,0:T(8,128)(2,1)}, u32[]{:S(2)}, u32[]{:S(2)}) %collective-permute-start.2) | collective-permute-done | bytes 29360160 | tf_op jit(solution)/shard_map/ppermute | solution.py:18
  43.6 10.0 %project.6.refs_8_ = f32[64,512]{1,0:T(8,128)} custom-call(s32[1]{0:T(128)} %bitcast.shard_ref, bf16[2,512,512]{2,1,0:T(8,128)(2,1)} %split_blocks.2.refs_0_, bf16[2,512,512]{2,1,0:T(8,128)(2,1)} %collective-permute-done.refs_1_, bf16[7168,2048]{1,0:T(8,128)(2,1)} %refs_4_.11, bf16[7168,2048]{1,0:T(8,128)(2,1)} %collective-permute-done.2.refs_3_.refs_5_, ...), custom_call_target="tpu_custom_call" | custom-call | flops 4294967296 | bytes 10485760 | tf_op jit(solution)/shard_map/project/pallas_call | solution.py:165
  53.6 2.7 %collective-permute-done.6.refs_0_ = bf16[2,512,512]{2,1,0:T(8,128)(2,1)} collective-permute-done((bf16[2,512,512]{2,1,0:T(8,128)(2,1)}, bf16[2,512,512]{2,1,0:T(8,128)(2,1)}, u32[]{:S(2)}, u32[]{:S(2)}) %collective-permute-start.6) | collective-permute-done | bytes 1048608 | tf_op jit(solution)/shard_map/ppermute | solution.py:18
  56.3 1.5 collective-permute-start.7
  57.8 1.5 collective-permute-start.11
  59.3 0.0 collective-permute-done.8.refs_2_
  59.3 0.0 collective-permute-done.9.refs_3_
  59.3 0.6 copy-done.8
  60.0 0.6 copy-done.9
  60.6 2.4 %pair_queries.1.refs_10_.refs_8_ = bf16[4096,128]{1,0:T(8,128)(2,1)} custom-call(bf16[64,1024]{1,0:T(8,128)(2,1)} %refs_0_, bf16[64,1024]{1,0:T(8,128)(2,1)} %copy-done.7, bf16[64,1024]{1,0:T(8,128)(2,1)} %copy-done.8, bf16[64,1024]{1,0:T(8,128)(2,1)} %copy-done.9), custom_call_target="tpu_custom_call" | custom-call | tf_op jit(solution)/shard_map/pair_queries/pallas_call | solution.py:262
  63.0 2.3 %collective-permute-done.1.refs_9_.refs_0_ = bf16[2,512,512]{2,1,0:T(8,128)(2,1)S(1)} collective-permute-done((bf16[2,512,512]{2,1,0:T(8,128)(2,1)}, bf16[2,512,512]{2,1,0:T(8,128)(2,1)S(1)}, u32[]{:S(2)}, u32[]{:S(2)}) %collective-permute-start.1) | collective-permute-done | bytes 1048608 | tf_op jit(solution)/shard_map/ppermute | solution.py:300
  65.3 0.0 collective-permute-start.3
  65.3 1.0 copy-done.1
  66.3 18.5 %project.7.refs_6_.refs_8_ = f32[64,512]{1,0:T(8,128)} custom-call(s32[1]{0:T(128)} %bitcast.shard_ref, bf16[2,512,512]{2,1,0:T(8,128)(2,1)} %split_blocks.2.refs_0_, bf16[2,512,512]{2,1,0:T(8,128)(2,1)} %collective-permute-done.refs_1_, bf16[7168,2048]{1,0:T(8,128)(2,1)} %refs_4_.11, bf16[7168,2048]{1,0:T(8,128)(2,1)} %collective-permute-done.2.refs_3_.refs_5_, ...), custom_call_target="tpu_custom_call" | custom-call | flops 10737418240 | bytes 26214400 | tf_op jit(solution)/shard_map/project/pallas_call | solution.py:165
  84.7 3.1 %collective-permute-done.7.refs_1_ = bf16[2,512,512]{2,1,0:T(8,128)(2,1)} collective-permute-done((bf16[2,512,512]{2,1,0:T(8,128)(2,1)}, bf16[2,512,512]{2,1,0:T(8,128)(2,1)}, u32[]{:S(2)}, u32[]{:S(2)}) %collective-permute-start.7) | collective-permute-done | bytes 1048608 | tf_op jit(solution)/shard_map/ppermute | solution.py:300
  87.9 22.8 %project.8.refs_9_.refs_8_ = f32[7168,512]{1,0:T(8,128)} custom-call(s32[1]{0:T(128)} %bitcast.shard_ref, bf16[2,512,512]{2,1,0:T(8,128)(2,1)} %collective-permute-done.6.refs_0_, bf16[2,512,512]{2,1,0:T(8,128)(2,1)} %collective-permute-done.7.refs_1_, bf16[7168,2048]{1,0:T(8,128)(2,1)} %refs_4_.11, ...), custom_call_target="tpu_custom_call" | custom-call | flops 15032385536 | bytes 36700160 | tf_op jit(solution)/shard_map/project/pallas_call | solution.py:165
  110.7 0.0 collective-permute-done.3.refs_1_
  110.7 13.0 %project.9.refs_8_ = f32[64,512]{1,0:T(8,128)} custom-call(s32[1]{0:T(128)} %bitcast.shard_ref, bf16[2,512,512]{2,1,0:T(8,128)(2,1)} %copy-done.1, bf16[2,512,512]{2,1,0:T(8,128)(2,1)} %collective-permute-done.3.refs_1_, bf16[7168,2048]{1,0:T(8,128)(2,1)} %refs_4_.11, bf16[7168,2048]{1,0:T(8,128)(2,1)} %collective-permute-done.2.refs_3_.refs_5_, ...), custom_call_target="tpu_custom_call" | custom-call | flops 6442450944 | bytes 15728640 | tf_op jit(solution)/shard_map/project/pallas_call | solution.py:165
  123.7 7.3 %collective-permute-done.10.refs_9_.refs_0_ = bf16[2,512,512]{2,1,0:T(8,128)(2,1)} collective-permute-done((bf16[2,512,512]{2,1,0:T(8,128)(2,1)}, bf16[2,512,512]{2,1,0:T(8,128)(2,1)}, u32[]{:S(2)}, u32[]{:S(2)}) %collective-permute-start.10) | collective-permute-done | bytes 1048608 | tf_op jit(solution)/shard_map/ppermute | solution.py:300
  131.1 0.0 collective-permute-start.15
  131.1 0.8 fusion
  131.8 1.6 collective-permute-start.17
  133.4 15.7 %project.10.refs_9_ = f32[64,512]{1,0:T(8,128)} custom-call(s32[1]{0:T(128)} %bitcast.shard_ref, bf16[2,512,512]{2,1,0:T(8,128)(2,1)} %copy-done.1, bf16[2,512,512]{2,1,0:T(8,128)(2,1)} %collective-permute-done.3.refs_1_, bf16[7168,2048]{1,0:T(8,128)(2,1)} %refs_4_.11, bf16[7168,2048]{1,0:T(8,128)(2,1)} %collective-permute-done.2.refs_3_.refs_5_, ...), custom_call_target="tpu_custom_call" | custom-call | flops 8589934592 | bytes 20971520 | tf_op jit(solution)/shard_map/project/pallas_call | solution.py:165
  149.1 0.9 pad_maximum_fusion.refs_0_
  150.0 1.6 collective-permute-done.11.refs_6_
  151.6 1.6 collective-permute-start.12
  153.2 1.4 collective-permute-start.13
  154.6 2.5 %collective-permute-start.14 = (f32[128,512]{1,0:T(8,128)S(1)}, f32[128,512]{1,0:T(8,128)}, u32[]{:S(2)}, u32[]{:S(2)}) collective-permute-start(f32[128,512]{1,0:T(8,128)S(1)} %pad_maximum_fusion.refs_0_), channel_id=1, source_target_pairs={{0,12},{1,13},{2,14},{3,15},{4,0},{5,1},{6,2},{7,3},{8,4},{9,5},{1... | collective-permute-start | bytes 786440 | tf_op jit(solution)/shard_map/ppermute | solution.py:317
  157.2 2.3 %collective-permute-done.15.refs_1_ = bf16[2,512,512]{2,1,0:T(8,128)(2,1)} collective-permute-done((bf16[2,512,512]{2,1,0:T(8,128)(2,1)}, bf16[2,512,512]{2,1,0:T(8,128)(2,1)}, u32[]{:S(2)}, u32[]{:S(2)}) %collective-permute-start.15) | collective-permute-done | bytes 1048608 | tf_op jit(solution)/shard_map/ppermute | solution.py:300
  159.5 1.5 collective-permute-start.16
  161.0 28.2 %project.11 = (f32[64,512]{1,0:T(8,128)}, f32[3072,512]{1,0:T(8,128)}) custom-call(s32[1]{0:T(128)} %bitcast.shard_ref, bf16[2,512,512]{2,1,0:T(8,128)(2,1)} %collective-permute-done.10.refs_9_.refs_0_, bf16[2,512,512]{2,1,0:T(8,128)(2,1)} %collective-permute-done.15.refs_1_, bf16[7168,2048]{1,0:T(8,128)(2,1)} %refs_4_.11, ...), custom_call_target="tpu_custom_call" | custom-call | flops 15032385536 | bytes 36700160 | tf_op jit(solution)/shard_map/project/pallas_call | solution.py:165
  189.2 3.3 %finish.3.before_ref = f32[64,512]{1,0:T(8,128)} custom-call(f32[3072,512]{1,0:T(8,128)} %get-tuple-element.42.hidden_ref, bf16[512,1024]{1,0:T(8,128)(2,1)} %collective-permute-done.4.gate_ref, bf16[64,7168]{1,0:T(8,128)(2,1)} %bitcast.9, f32[64,512]{1,0:T(8,128)} %get-tuple-element.46.before_ref), custom_call_target="tpu_custom_call" | custom-call | tf_op jit(solution)/shard_map/finish/pallas_call | solution.py:209
  192.5 0.0 collective-permute-done.17.gate_ref
  192.5 4.9 %finish.4.before_ref = f32[64,512]{1,0:T(8,128)} custom-call(f32[3072,512]{1,0:T(8,128)} %get-tuple-element.42.hidden_ref, bf16[512,1536]{1,0:T(8,128)(2,1)} %collective-permute-done.17.gate_ref, bf16[64,7168]{1,0:T(8,128)(2,1)} %bitcast.10, f32[64,512]{1,0:T(8,128)} %finish.3.before_ref), custom_call_target="tpu_custom_call" | custom-call | tf_op jit(solution)/shard_map/finish/pallas_call | solution.py:209
  197.4 0.0 collective-permute-done.16.gate_ref
  197.4 2.5 %finish.5 = bf16[64,512]{1,0:T(8,128)(2,1)} custom-call(f32[3072,512]{1,0:T(8,128)} %get-tuple-element.42.hidden_ref, bf16[512,512]{1,0:T(8,128)(2,1)} %collective-permute-done.16.gate_ref, bf16[64,7168]{1,0:T(8,128)(2,1)} %bitcast.11, f32[64,512]{1,0:T(8,128)} %finish.4.before_ref), custom_call_target="tpu_custom_call" | custom-call | tf_op jit(solution)/shard_map/finish/pallas_call | solution.py:209
  199.9 0.5 collective-permute-start.18
  200.4 0.0 collective-permute-start.19
  200.4 0.0 collective-permute-done.12.refs_1_
  200.4 1.6 collective-permute-start.20
  202.1 3.2 %collective-permute-start.21 = (bf16[64,512]{1,0:T(8,128)(2,1)}, bf16[64,512]{1,0:T(8,128)(2,1)S(1)}, u32[]{:S(2)}, u32[]{:S(2)}) collective-permute-start(bf16[64,512]{1,0:T(8,128)(2,1)} %finish.5), channel_id=1, source_target_pairs={{0,14},{1,15},{2,12},{3,13},{4,2},{5,3},{6,0},{7,1},{8,6},{9,7},{1... | collective-permute-start | bytes 196616 | tf_op jit(solution)/shard_map/ppermute | solution.py:317
  205.2 0.0 collective-permute-done.14.refs_3_
  205.2 0.0 collective-permute-done.18.refs_4_
  205.2 2.4 %collective-permute-done.19.refs_5_ = bf16[64,512]{1,0:T(8,128)(2,1)S(1)} collective-permute-done((bf16[64,512]{1,0:T(8,128)(2,1)}, bf16[64,512]{1,0:T(8,128)(2,1)S(1)}, u32[]{:S(2)}, u32[]{:S(2)}) %collective-permute-start.19) | collective-permute-done | bytes 65568 | tf_op jit(solution)/shard_map/ppermute | solution.py:317
  207.6 1.5 collective-permute-done.21.refs_7_
  209.2 0.6 copy-done.13
  209.8 3.6 %score.1 = f32[64,512]{1,0:T(8,128)} custom-call(f32[128,512]{1,0:T(8,128)} %copy-done.4, f32[128,512]{1,0:T(8,128)} %collective-permute-done.12.refs_1_, f32[128,512]{1,0:T(8,128)} %collective-permute-done.13.refs_2_, f32[128,512]{1,0:T(8,128)} %collective-permute-done.14.refs_3_, bf16[64,512]{1,0:T(8,128)(2,1)} %copy-done.10, bf16[64,512]{1,0:T(8,128)(2,1)} %copy-done.11, ...), custom_call_target="tpu_custom_call" | custom-call | tf_op jit(solution)/shard_map/score/pallas_call | solution.py:272
  (27 shorter events, 0.1 us)
Async XLA Ops:
  0.0 131.1 %copy-start = (bf16[512,2048]{1,0:T(8,128)(2,1)S(1)}, bf16[512,2048]{1,0:T(8,128)(2,1)}, u32[]{:S(2)}) copy-start(bf16[512,2048]{1,0:T(8,128)(2,1)} %param.7) | copy-start | bytes 6291460
  0.0 11.5 %copy-start.6 = (bf16[64,1024]{1,0:T(8,128)(2,1)S(1)}, bf16[64,1024]{1,0:T(8,128)(2,1)}, u32[]{:S(2)}) copy-start(bf16[64,1024]{1,0:T(8,128)(2,1)} %refs_0_) | copy-start | bytes 393220
  0.0 43.6 %collective-permute-start.2 = (bf16[7168,2048]{1,0:T(8,128)(2,1)}, bf16[7168,2048]{1,0:T(8,128)(2,1)}, u32[]{:S(2)}, u32[]{:S(2)}) collective-permute-start(bf16[7168,2048]{1,0:T(8,128)(2,1)} %refs_4_.11), channel_id=1, source_target_pairs={{0,1},{1,0},{2,3},{3,2},{4,5},{5,4},{6,7},{7,6},{8,9},{9,8},{10,11... | collective-permute-start | bytes 88080392 | tf_op jit(solution)/shard_map/ppermute | solution.py:18
  1.8 2.8 %copy-start.2 = (bf16[512,1024]{1,0:T(8,128)(2,1)}, bf16[512,1024]{1,0:T(8,128)(2,1)S(1)}, u32[]{:S(2)}) copy-start(bf16[512,1024]{1,0:T(8,128)(2,1)S(1)} %slice.12.refs_0_) | copy-start | bytes 3145732
  1.8 29.2 %collective-permute-start.4 = (bf16[512,1024]{1,0:T(8,128)(2,1)S(1)}, bf16[512,1024]{1,0:T(8,128)(2,1)}, u32[]{:S(2)}, u32[]{:S(2)}) collective-permute-start(bf16[512,1024]{1,0:T(8,128)(2,1)S(1)} %slice.12.refs_0_), channel_id=1, source_target_pairs={{0,2},{1,3},{2,0},{3,1},{4,6},{5,7},{6,4},{7,5},{8,10},{9,11},{10,... | collective-permute-start | bytes 3145736 | tf_op jit(solution)/shard_map/ppermute | solution.py:18
  9.9 27.3 %collective-permute-start = (bf16[2,512,512]{2,1,0:T(8,128)(2,1)}, bf16[2,512,512]{2,1,0:T(8,128)(2,1)}, u32[]{:S(2)}, u32[]{:S(2)}) collective-permute-start(bf16[2,512,512]{2,1,0:T(8,128)(2,1)} %split_blocks.2.refs_0_), channel_id=1, source_target_pairs={{0,4},{4,8},{8,12},{12,0},{1,5},{5,9},{9,13},{13,1},{2,6},{6,10},{... | collective-permute-start | bytes 3145736 | tf_op jit(solution)/shard_map/ppermute | solution.py:300
  11.5 19.5 %collective-permute-start.5 = (bf16[64,1024]{1,0:T(8,128)(2,1)S(1)}, bf16[64,1024]{1,0:T(8,128)(2,1)S(1)}, u32[]{:S(2)}, u32[]{:S(2)}) collective-permute-start(bf16[64,1024]{1,0:T(8,128)(2,1)S(1)} %copy-done.6), channel_id=1, source_target_pairs={{0,2},{1,3},{2,0},{3,1},{4,6},{5,7},{6,4},{7,5},{8,10},{9,11},{10,... | collective-permute-start | bytes 393224 | tf_op jit(solution)/shard_map/ppermute | solution.py:18
  31.0 22.6 %copy-start.7 = (bf16[64,1024]{1,0:T(8,128)(2,1)}, bf16[64,1024]{1,0:T(8,128)(2,1)S(1)}, u32[]{:S(2)}) copy-start(bf16[64,1024]{1,0:T(8,128)(2,1)S(1)} %collective-permute-done.5.refs_1_) | copy-start | bytes 393220
  31.0 25.3 %collective-permute-start.6 = (bf16[2,512,512]{2,1,0:T(8,128)(2,1)}, bf16[2,512,512]{2,1,0:T(8,128)(2,1)}, u32[]{:S(2)}, u32[]{:S(2)}) collective-permute-start(bf16[2,512,512]{2,1,0:T(8,128)(2,1)} %split_blocks.3), channel_id=1, source_target_pairs={{0,2},{1,3},{2,0},{3,1},{4,6},{5,7},{6,4},{7,5},{8,10},{9,11},{10,... | collective-permute-start | bytes 3145736 | tf_op jit(solution)/shard_map/ppermute | solution.py:18
  37.2 28.1 %collective-permute-start.1 = (bf16[2,512,512]{2,1,0:T(8,128)(2,1)}, bf16[2,512,512]{2,1,0:T(8,128)(2,1)S(1)}, u32[]{:S(2)}, u32[]{:S(2)}) collective-permute-start(bf16[2,512,512]{2,1,0:T(8,128)(2,1)} %collective-permute-done.refs_1_), channel_id=1, source_target_pairs={{0,4},{4,8},{8,12},{12,0},{1,5},{5,9},{9,13},{13,1},{2,6},{6,10},{... | collective-permute-start | bytes 3145736 | tf_op jit(solution)/shard_map/ppermute | solution.py:300
  37.2 22.1 %collective-permute-start.8 = (bf16[64,1024]{1,0:T(8,128)(2,1)S(1)}, bf16[64,1024]{1,0:T(8,128)(2,1)S(1)}, u32[]{:S(2)}, u32[]{:S(2)}) collective-permute-start(bf16[64,1024]{1,0:T(8,128)(2,1)S(1)} %copy-done.6), channel_id=1, source_target_pairs={{0,1},{1,0},{2,3},{3,2},{4,5},{5,4},{6,7},{7,6},{8,9},{9,8},{10,11... | collective-permute-start | bytes 393224 | tf_op jit(solution)/shard_map/ppermute | solution.py:18
  37.2 22.1 %collective-permute-start.9 = (bf16[64,1024]{1,0:T(8,128)(2,1)S(1)}, bf16[64,1024]{1,0:T(8,128)(2,1)S(1)}, u32[]{:S(2)}, u32[]{:S(2)}) collective-permute-start(bf16[64,1024]{1,0:T(8,128)(2,1)S(1)} %collective-permute-done.5.refs_1_), channel_id=1, source_target_pairs={{0,1},{1,0},{2,3},{3,2},{4,5},{5,4},{6,7},{7,6},{8,9},{9,8},{10,11... | collective-permute-start | bytes 393224 | tf_op jit(solution)/shard_map/ppermute | solution.py:18
  56.3 31.6 %collective-permute-start.7 = (bf16[2,512,512]{2,1,0:T(8,128)(2,1)}, bf16[2,512,512]{2,1,0:T(8,128)(2,1)}, u32[]{:S(2)}, u32[]{:S(2)}) collective-permute-start(bf16[2,512,512]{2,1,0:T(8,128)(2,1)} %collective-permute-done.6.refs_0_), channel_id=1, source_target_pairs={{0,4},{4,8},{8,12},{12,0},{1,5},{5,9},{9,13},{13,1},{2,6},{6,10},{... | collective-permute-start | bytes 3145736 | tf_op jit(solution)/shard_map/ppermute | solution.py:300
  57.8 93.8 %collective-permute-start.11 = (bf16[512,4096]{1,0:T(8,128)(2,1)}, bf16[512,4096]{1,0:T(8,128)(2,1)}, u32[]{:S(2)}, u32[]{:S(2)}) collective-permute-start(bf16[512,4096]{1,0:T(8,128)(2,1)} %slice.13), channel_id=1, source_target_pairs={{0,2},{1,3},{2,0},{3,1},{4,6},{5,7},{6,4},{7,5},{8,10},{9,11},{10,... | collective-permute-start | bytes 12582920 | tf_op jit(solution)/shard_map/ppermute | solution.py:18
  59.3 0.6 copy-start.8
  60.0 0.6 copy-start.9
  65.3 1.0 copy-start.1
  65.3 45.4 %collective-permute-start.3 = (bf16[2,512,512]{2,1,0:T(8,128)(2,1)S(1)}, bf16[2,512,512]{2,1,0:T(8,128)(2,1)}, u32[]{:S(2)}, u32[]{:S(2)}) collective-permute-start(bf16[2,512,512]{2,1,0:T(8,128)(2,1)S(1)} %collective-permute-done.1.refs_9_.refs_0_), channel_id=1, source_target_pairs={{0,4},{4,8},{8,12},{12,0},{1,5},{5,9},{9,13},{13,1},{2,6},{6,10},{... | collective-permute-start | bytes 3145736 | tf_op jit(solution)/shard_map/ppermute | solution.py:300
  87.9 43.2 %collective-permute-start.10 = (bf16[2,512,512]{2,1,0:T(8,128)(2,1)}, bf16[2,512,512]{2,1,0:T(8,128)(2,1)}, u32[]{:S(2)}, u32[]{:S(2)}) collective-permute-start(bf16[2,512,512]{2,1,0:T(8,128)(2,1)} %collective-permute-done.7.refs_1_), channel_id=1, source_target_pairs={{0,4},{4,8},{8,12},{12,0},{1,5},{5,9},{9,13},{13,1},{2,6},{6,10},{... | collective-permute-start | bytes 3145736 | tf_op jit(solution)/shard_map/ppermute | solution.py:300
  110.7 20.4 %copy-start.5 = (bf16[2048,64]{0,1:T(8,128)(2,1)S(1)}, bf16[2048,64]{0,1:T(8,128)(2,1)}, u32[]{:S(2)}) copy-start(bf16[2048,64]{0,1:T(8,128)(2,1)} %param.11) | copy-start | bytes 786436
  110.7 21.1 %copy-start.3 = (bf16[512,1536]{1,0:T(8,128)(2,1)S(1)}, bf16[512,1536]{1,0:T(8,128)(2,1)}, u32[]{:S(2)}) copy-start(bf16[512,1536]{1,0:T(8,128)(2,1)} %slice.14) | copy-start | bytes 4718596
  131.1 28.4 %collective-permute-start.15 = (bf16[2,512,512]{2,1,0:T(8,128)(2,1)}, bf16[2,512,512]{2,1,0:T(8,128)(2,1)}, u32[]{:S(2)}, u32[]{:S(2)}) collective-permute-start(bf16[2,512,512]{2,1,0:T(8,128)(2,1)} %collective-permute-done.10.refs_9_.refs_0_), channel_id=1, source_target_pairs={{0,4},{4,8},{8,12},{12,0},{1,5},{5,9},{9,13},{13,1},{2,6},{6,10},{... | collective-permute-start | bytes 3145736 | tf_op jit(solution)/shard_map/ppermute | solution.py:300
  131.8 60.6 %collective-permute-start.17 = (bf16[512,1536]{1,0:T(8,128)(2,1)S(1)}, bf16[512,1536]{1,0:T(8,128)(2,1)}, u32[]{:S(2)}, u32[]{:S(2)}) collective-permute-start(bf16[512,1536]{1,0:T(8,128)(2,1)S(1)} %copy-done.3), channel_id=1, source_target_pairs={{0,2},{1,3},{2,0},{3,1},{4,6},{5,7},{6,4},{7,5},{8,10},{9,11},{10,... | collective-permute-start | bytes 4718600 | tf_op jit(solution)/shard_map/ppermute | solution.py:18
  150.0 39.2 %copy-start.4 = (f32[128,512]{1,0:T(8,128)}, f32[128,512]{1,0:T(8,128)S(1)}, u32[]{:S(2)}) copy-start(f32[128,512]{1,0:T(8,128)S(1)} %pad_maximum_fusion.refs_0_) | copy-start | bytes 786436
  151.6 48.8 %collective-permute-start.12 = (f32[128,512]{1,0:T(8,128)S(1)}, f32[128,512]{1,0:T(8,128)}, u32[]{:S(2)}, u32[]{:S(2)}) collective-permute-start(f32[128,512]{1,0:T(8,128)S(1)} %pad_maximum_fusion.refs_0_), channel_id=1, source_target_pairs={{0,4},{1,5},{2,6},{3,7},{4,8},{5,9},{6,10},{7,11},{8,12},{9,13},{1... | collective-permute-start | bytes 786440 | tf_op jit(solution)/shard_map/ppermute | solution.py:317
  153.2 48.8 %collective-permute-start.13 = (f32[128,512]{1,0:T(8,128)S(1)}, f32[128,512]{1,0:T(8,128)}, u32[]{:S(2)}, u32[]{:S(2)}) collective-permute-start(f32[128,512]{1,0:T(8,128)S(1)} %pad_maximum_fusion.refs_0_), channel_id=1, source_target_pairs={{0,8},{1,9},{2,10},{3,11},{4,12},{5,13},{6,14},{7,15},{8,0},{9,1},... | collective-permute-start | bytes 786440 | tf_op jit(solution)/shard_map/ppermute | solution.py:317
  154.6 50.6 %collective-permute-start.14 = (f32[128,512]{1,0:T(8,128)S(1)}, f32[128,512]{1,0:T(8,128)}, u32[]{:S(2)}, u32[]{:S(2)}) collective-permute-start(f32[128,512]{1,0:T(8,128)S(1)} %pad_maximum_fusion.refs_0_), channel_id=1, source_target_pairs={{0,12},{1,13},{2,14},{3,15},{4,0},{5,1},{6,2},{7,3},{8,4},{9,5},{1... | collective-permute-start | bytes 786440 | tf_op jit(solution)/shard_map/ppermute | solution.py:317
  159.5 37.9 %collective-permute-start.16 = (bf16[512,512]{1,0:T(8,128)(2,1)}, bf16[512,512]{1,0:T(8,128)(2,1)}, u32[]{:S(2)}, u32[]{:S(2)}) collective-permute-start(bf16[512,512]{1,0:T(8,128)(2,1)} %slice.15), channel_id=1, source_target_pairs={{0,2},{1,3},{2,0},{3,1},{4,6},{5,7},{6,4},{7,5},{8,10},{9,11},{10,... | collective-permute-start | bytes 1572872 | tf_op jit(solution)/shard_map/ppermute | solution.py:18
  199.9 5.3 %collective-permute-start.18 = (bf16[64,512]{1,0:T(8,128)(2,1)}, bf16[64,512]{1,0:T(8,128)(2,1)S(1)}, u32[]{:S(2)}, u32[]{:S(2)}) collective-permute-start(bf16[64,512]{1,0:T(8,128)(2,1)} %finish.5), channel_id=1, source_target_pairs={{0,2},{1,3},{2,0},{3,1},{4,6},{5,7},{6,4},{7,5},{8,10},{9,11},{10,... | collective-permute-start | bytes 196616 | tf_op jit(solution)/shard_map/ppermute | solution.py:317
  200.4 7.2 %collective-permute-start.19 = (bf16[64,512]{1,0:T(8,128)(2,1)}, bf16[64,512]{1,0:T(8,128)(2,1)S(1)}, u32[]{:S(2)}, u32[]{:S(2)}) collective-permute-start(bf16[64,512]{1,0:T(8,128)(2,1)} %finish.5), channel_id=1, source_target_pairs={{0,6},{1,7},{2,4},{3,5},{4,10},{5,11},{6,8},{7,9},{8,14},{9,15},{1... | collective-permute-start | bytes 196616 | tf_op jit(solution)/shard_map/ppermute | solution.py:317
  200.4 7.2 %collective-permute-start.20 = (bf16[64,512]{1,0:T(8,128)(2,1)}, bf16[64,512]{1,0:T(8,128)(2,1)S(1)}, u32[]{:S(2)}, u32[]{:S(2)}) collective-permute-start(bf16[64,512]{1,0:T(8,128)(2,1)} %finish.5), channel_id=1, source_target_pairs={{0,10},{1,11},{2,8},{3,9},{4,14},{5,15},{6,12},{7,13},{8,2},{9,3},... | collective-permute-start | bytes 196616 | tf_op jit(solution)/shard_map/ppermute | solution.py:317
  202.1 7.1 %collective-permute-start.21 = (bf16[64,512]{1,0:T(8,128)(2,1)}, bf16[64,512]{1,0:T(8,128)(2,1)S(1)}, u32[]{:S(2)}, u32[]{:S(2)}) collective-permute-start(bf16[64,512]{1,0:T(8,128)(2,1)} %finish.5), channel_id=1, source_target_pairs={{0,14},{1,15},{2,12},{3,13},{4,2},{5,3},{6,0},{7,1},{8,6},{9,7},{1... | collective-permute-start | bytes 196616 | tf_op jit(solution)/shard_map/ppermute | solution.py:317
  205.2 3.9 %copy-start.10 = (bf16[64,512]{1,0:T(8,128)(2,1)}, bf16[64,512]{1,0:T(8,128)(2,1)S(1)}, u32[]{:S(2)}) copy-start(bf16[64,512]{1,0:T(8,128)(2,1)S(1)} %collective-permute-done.18.refs_4_) | copy-start | bytes 196612
  207.6 1.6 copy-start.11
  207.6 1.6 copy-start.12
  209.2 0.6 copy-start.13

commit v3 on v2

--- a/solution.py
+++ b/solution.py
@@ -52,7 +52,7 @@
     return jnp.dot(proj_ref[...], up_grad, preferred_element_type=jnp.float32)
 
 
-def project_kernel(tiles, ahead, pieces, chained, carried, shard_ref, *refs):
+def project_kernel(tiles, ahead, pieces, chained, carried, tailed, shard_ref, *refs):
     refs = list(refs)
     take = lambda n: [refs.pop(0) for _ in range(n)]
     grads = take(pieces)
@@ -60,8 +60,8 @@
     gate_ref, proj_ref = take(2) if tiles else (None, None)
     (before_ref,) = take(1) if chained else (None,)
     (partial_ref,) = take(1) if carried else (None,)
+    (tail_ref,) = take(1) if tailed else (None,)
     sum_ref = refs.pop() if tiles else None
-    odd_ref, even_ref = [refs.pop() for _ in range(2)] if tiles and ahead else (None, None)
     later_ref = refs.pop() if ahead else None
     out_ref = refs.pop() if tiles else None
     step = pl.program_id(0)
@@ -76,56 +76,36 @@
                 hidden = term if hidden is None else hidden + term
         return hidden
 
-    def multiply(hidden_ref):
-        hidden_ref[...] = product()
-
     if not tiles:
-        multiply(later_ref)
+        later_ref[...] = product()
         return
 
-    def reduce(hidden_ref):
-        sum_ref[...] += gated(hidden_ref[...], gate_ref, proj_ref)
-
     @pl.when(step == 0)
     def _():
         sum_ref[...] = before_ref[...] if chained else jnp.zeros_like(sum_ref)
 
-    if not ahead:
+    @pl.when(step < tiles)
+    def _():
         sum_ref[...] += gated(product(), gate_ref, proj_ref)
 
-        @pl.when(step == tiles - 1)
+    if ahead:
+
+        @pl.when((step >= tiles) & (step < tiles + ahead))
         def _():
-            out_ref[...] = sum_ref[...]
-
-        return
-
-    @pl.when(step == 0)
-    def _():
-        odd_ref[...] = jnp.zeros_like(odd_ref)
-
-    @pl.when((step < tiles) & (lax.rem(step, 2) == 0))
-    def _():
-        reduce(odd_ref)
-        multiply(even_ref)
-
-    if tiles > 1:
-
-        @pl.when((step < tiles) & (lax.rem(step, 2) == 1))
+            later_ref[...] = product()
+
+    if tailed:
+
+        @pl.when(step == tiles + ahead)
         def _():
-            reduce(even_ref)
-            multiply(odd_ref)
-
-    @pl.when(step == tiles)
-    def _():
-        reduce(even_ref if tiles % 2 else odd_ref)
+            sum_ref[...] += gated(product(), tail_ref, proj_ref)
+
+    @pl.when(step == tiles + ahead + tailed - 1)
+    def _():
         out_ref[...] = sum_ref[...]
 
-    @pl.when(step >= tiles)
-    def _():
-        multiply(later_ref)
-
-
-def project(shard, grads, gate, weights, proj, offset, span, extra, gate_column, before, partial, after):
+
+def project(shard, grads, gate, weights, proj, offset, span, extra, gate_column, before, partial, after, tail=None):
     places = [place for place, _ in grads]
     pieces = [piece for _, piece in grads]
     _, width, rows = pieces[0].shape
@@ -134,11 +114,13 @@
     tile = TILE if (span + extra) % TILE == 0 else span + extra
     tiles, ahead = span // tile, extra // tile
     first, gate_first = offset // tile, gate_column // tile
-    now = lambda i: jnp.minimum(i, tiles + ahead - 1)
-    last = lambda i: jnp.clip(i - 1, 0, tiles - 1) if ahead else i
+    tailed = int(tail is not None)
+    now = lambda i: i
+    last = lambda i: jnp.minimum(i, tiles - 1)
+    ends = lambda i: jnp.where(i < tiles + ahead, jnp.minimum(i, tiles - 1), i)
     chained, carried = before is not None, partial is not None
     total = pl.BlockSpec((k, rows), lambda i, s: (0, 0))
-    later = pl.BlockSpec((tile, rows), lambda i, s: (jnp.maximum(i - tiles, 0), 0))
+    later = pl.BlockSpec((tile, rows), lambda i, s: (jnp.clip(i - tiles, 0, ahead - 1), 0))
 
     def weight_spec(place):
         return pl.BlockSpec(
@@ -151,7 +133,7 @@
     if tiles:
         specs += [
             pl.BlockSpec((rows, tile), lambda i, s: (0, gate_first + last(i))),
-            pl.BlockSpec((k, tile), lambda i, s: (0, first + last(i))),
+            pl.BlockSpec((k, tile), lambda i, s: (0, first + ends(i))),
         ]
         operands += [gate, proj]
     if chained:
@@ -160,17 +142,18 @@
     if carried:
         specs.append(pl.BlockSpec((tile, rows), lambda i, s: (first + now(i), 0)))
         operands.append(partial)
-    hidden = pltpu.VMEM((tile, rows), jnp.float32)
+    if tailed:
+        specs.append(pl.BlockSpec((rows, tile), lambda i, s: (0, 0)))
+        operands.append(tail)
     depth = 2 * width * len(pieces)
     return pl.pallas_call(
-        functools.partial(project_kernel, tiles, ahead, len(pieces), chained, carried),
+        functools.partial(project_kernel, tiles, ahead, len(pieces), chained, carried, tailed),
         grid_spec=pltpu.PrefetchScalarGridSpec(
             num_scalar_prefetch=1,
-            grid=(tiles + ahead,),
+            grid=(tiles + ahead + tailed,),
             in_specs=specs + [ANY] * len(after),
             out_specs=[total] * bool(tiles) + [later] * bool(ahead),
-            scratch_shapes=[hidden, hidden] * bool(tiles and ahead)
-            + [pltpu.VMEM((k, rows), jnp.float32)] * bool(tiles),
+            scratch_shapes=[pltpu.VMEM((k, rows), jnp.float32)] * bool(tiles),
         ),
         out_shape=[jax.ShapeDtypeStruct((k, rows), jnp.float32)] * bool(tiles)
         + [jax.ShapeDtypeStruct((extra, rows), jnp.float32)] * bool(ahead),
@@ -399,12 +382,11 @@
         final_gate, own_sum = lax.optimization_barrier((parts[-1], own_sum))
         last_gates.append(swap(final_gate, "dp", n_dp, far))
     far_sum, *later = project(
-        shard, far_late, far_gate, weights, proj_out, 0, main, sum(spans), 0, None, partial, (own_sum,)
+        shard, far_late, far_gate, weights, proj_out, 0, main, sum(spans[:-1]), 0, None, partial, (own_sum,), start_gate
     )
     if later:
-        order = [len(spans) - 1] + list(range(len(spans) - 1))
-        for k, gate in zip(order, [start_gate] + last_gates):
-            final = k == order[-1]
+        for k, gate in enumerate(last_gates):
+            final = k == len(last_gates) - 1
             far_sum = finish(
                 later[0],
                 offsets[k] - main,

time: 214 us -> 212 us (level)
  Pallas kernels: 136 us -> 131 us
  starting transfers between devices: 24.8 us -> 27.3 us
    pallas_call x3 -> x2, Pallas kernels: 10.7 us -> 7.45 us  [finish(): pl.pallas_call(finish_kernel, grid=(span // SMALL,), in_specs=[pl.BlockSp...]
    ppermute x7, starting transfers between devices: 10.8 us -> 13.4 us  [spread(): got.append(lax.ppermute(value, ('tensor', 'dp'), pairs))]
  transfers between devices with their start and end apart: 22 -> 22, of which waited for: 11 -> 13; matrix products, arithmetic and copies ran while one was open for 6% -> 6% of each run, Pallas kernels for 62% -> 60%
where the time goes in v3:
time: 212 us
  Pallas kernels  131 us (62%)
  waiting for transfers between devices  37.5 us (18%)
  starting transfers between devices  27.3 us (13%)
  local copies, waits for them, and re-layouts  13.6 us (6%)
    pallas_call x6, Pallas kernels, project(): pl.pallas_call(functools.partial(project_kernel, tiles, ahead, len(pieces...  107 us
    ppermute x6, waiting for transfers between devices, onward(): lax.ppermute(piece, 'tensor', [(i, (i + 1) % n_tensor) for i in range(n_t...  19.2 us
    ppermute x9, waiting for transfers between devices, swap(): return lax.ppermute(value, axis, [(i, i ^ mask) for i in range(size)])  15.5 us
    ppermute x7, starting transfers between devices, spread(): got.append(lax.ppermute(value, ('tensor', 'dp'), pairs))  13.4 us
    ppermute x9, starting transfers between devices, swap(): return lax.ppermute(value, axis, [(i, i ^ mask) for i in range(size)])  10.9 us
    pallas_call x2, Pallas kernels, split_blocks(): pl.pallas_call(functools.partial(split_kernel, first), grid=(4,), in_spec...  10.7 us
    slice x4, local copies, waits for them, and re-layouts, on_device(): cut = lambda source, offset, span: source[:, offset:offset + span]  10.6 us
    pallas_call x2, Pallas kernels, finish(): pl.pallas_call(finish_kernel, grid=(span // SMALL,), in_specs=[pl.BlockSp...  7.45 us
  transfers between devices with their start and end apart: 22, of which 13 were waited for; matrix products, arithmetic and copies ran while one was open for 6% of the time, Pallas kernels for 60%

profile of v3, /device:TPU:0, one launch (start us, length us, event | category | flops | bytes accessed | tf_op | source)
XLA Modules:
  0.0 211.7 jit_solution(11802205030044555544)
XLA Ops:
  0.0 0.5 collective-permute-start.2
  0.5 1.3 slice.12.refs_0_
  1.8 2.7 %collective-permute-start.4 = (bf16[512,1024]{1,0:T(8,128)(2,1)S(1)}, bf16[512,1024]{1,0:T(8,128)(2,1)}, u32[]{:S(2)}, u32[]{:S(2)}) collective-permute-start(bf16[512,1024]{1,0:T(8,128)(2,1)S(1)} %slice.12.refs_0_), channel_id=1, source_target_pairs={{0,2},{1,3},{2,0},{3,1},{4,6},{5,7},{6,4},{7,5},{8,10},{9,11},{10,... | collective-permute-start | bytes 3145736 | tf_op jit(solution)/shard_map/ppermute | solution.py:18
  4.5 5.3 %split_blocks.2.refs_0_ = bf16[2,512,512]{2,1,0:T(8,128)(2,1)} custom-call(bf16[512,4,512]{2,1,0:T(4,128)(2,1)} %grad_ref.3, bf16[512,1024]{1,0:T(8,128)(2,1)} %copy-done.2), custom_call_target="tpu_custom_call" | custom-call | tf_op jit(solution)/shard_map/split_blocks/pallas_call | solution.py:37
  9.9 1.6 collective-permute-start
  11.4 0.9 collective-permute-start.5
  12.3 4.7 %slice.13 = bf16[512,4096]{1,0:T(8,128)(2,1)} slice(bf16[512,7168]{1,0:T(8,128)(2,1)} %refs_6_.7), slice={[0:512], [0:4096]} | slice | bytes 8388608 | tf_op jit(solution)/shard_map/slice | solution.py:305
  17.1 2.7 %slice.14 = bf16[512,1536]{1,0:T(8,128)(2,1)} slice(bf16[512,7168]{1,0:T(8,128)(2,1)} %refs_6_.7), slice={[0:512], [4096:5632]} | slice | bytes 3145728 | tf_op jit(solution)/shard_map/slice | solution.py:305
  19.8 1.9 slice.15
  21.6 5.4 %split_blocks.3 = bf16[2,512,512]{2,1,0:T(8,128)(2,1)} custom-call(bf16[512,4,512]{2,1,0:T(4,128)(2,1)} %grad_ref.3, bf16[2,512,512]{2,1,0:T(8,128)(2,1)} %split_blocks.2.refs_0_), custom_call_target="tpu_custom_call" | custom-call | tf_op jit(solution)/shard_map/split_blocks/pallas_call | solution.py:37
  27.0 4.0 %collective-permute-done.5.refs_1_ = bf16[64,1024]{1,0:T(8,128)(2,1)S(1)} collective-permute-done((bf16[64,1024]{1,0:T(8,128)(2,1)S(1)}, bf16[64,1024]{1,0:T(8,128)(2,1)S(1)}, u32[]{:S(2)}, u32[]{:S(2)}) %collective-permute-start.5) | collective-permute-done | bytes 131104 | tf_op jit(solution)/shard_map/ppermute | solution.py:18
  31.0 0.0 collective-permute-done.4.refs_9_
  31.0 1.7 collective-permute-start.6
  32.7 4.4 %collective-permute-done.refs_1_ = bf16[2,512,512]{2,1,0:T(8,128)(2,1)} collective-permute-done((bf16[2,512,512]{2,1,0:T(8,128)(2,1)}, bf16[2,512,512]{2,1,0:T(8,128)(2,1)}, u32[]{:S(2)}, u32[]{:S(2)}) %collective-permute-start) | collective-permute-done | bytes 1048608 | tf_op jit(solution)/shard_map/ppermute | solution.py:283
  37.1 0.0 collective-permute-start.1
  37.2 0.0 collective-permute-start.8
  37.2 0.5 collective-permute-start.9
  37.7 5.9 %collective-permute-done.2.refs_3_.refs_5_ = bf16[7168,2048]{1,0:T(8,128)(2,1)} collective-permute-done((bf16[7168,2048]{1,0:T(8,128)(2,1)}, bf16[7168,2048]{1,0:T(8,128)(2,1)}, u32[]{:S(2)}, u32[]{:S(2)}) %collective-permute-start.2) | collective-permute-done | bytes 29360160 | tf_op jit(solution)/shard_map/ppermute | solution.py:18
  43.6 10.1 %project.6.refs_8_ = f32[64,512]{1,0:T(8,128)} custom-call(s32[1]{0:T(128)} %bitcast.shard_ref, bf16[2,512,512]{2,1,0:T(8,128)(2,1)} %split_blocks.2.refs_0_, bf16[2,512,512]{2,1,0:T(8,128)(2,1)} %collective-permute-done.refs_1_, bf16[7168,2048]{1,0:T(8,128)(2,1)} %refs_4_.11, bf16[7168,2048]{1,0:T(8,128)(2,1)} %collective-permute-done.2.refs_3_.refs_5_, ...), custom_call_target="tpu_custom_call" | custom-call | flops 4294967296 | bytes 10485760 | tf_op jit(solution)/shard_map/project/pallas_call | solution.py:149
  53.6 2.7 %collective-permute-done.6.refs_0_ = bf16[2,512,512]{2,1,0:T(8,128)(2,1)} collective-permute-done((bf16[2,512,512]{2,1,0:T(8,128)(2,1)}, bf16[2,512,512]{2,1,0:T(8,128)(2,1)}, u32[]{:S(2)}, u32[]{:S(2)}) %collective-permute-start.6) | collective-permute-done | bytes 1048608 | tf_op jit(solution)/shard_map/ppermute | solution.py:18
  56.3 1.5 collective-permute-start.7
  57.8 1.5 collective-permute-start.11
  59.3 0.0 collective-permute-done.8.refs_2_
  59.3 0.0 collective-permute-done.9.refs_3_
  59.3 0.7 copy-done.8
  60.0 0.7 copy-done.9
  60.7 2.4 %pair_queries.1.refs_10_.refs_8_ = bf16[4096,128]{1,0:T(8,128)(2,1)} custom-call(bf16[64,1024]{1,0:T(8,128)(2,1)} %refs_0_, bf16[64,1024]{1,0:T(8,128)(2,1)} %copy-done.7, bf16[64,1024]{1,0:T(8,128)(2,1)} %copy-done.8, bf16[64,1024]{1,0:T(8,128)(2,1)} %copy-done.9), custom_call_target="tpu_custom_call" | custom-call | tf_op jit(solution)/shard_map/pair_queries/pallas_call | solution.py:245
  63.0 2.2 %collective-permute-done.1.refs_9_.refs_0_ = bf16[2,512,512]{2,1,0:T(8,128)(2,1)S(1)} collective-permute-done((bf16[2,512,512]{2,1,0:T(8,128)(2,1)}, bf16[2,512,512]{2,1,0:T(8,128)(2,1)S(1)}, u32[]{:S(2)}, u32[]{:S(2)}) %collective-permute-start.1) | collective-permute-done | bytes 1048608 | tf_op jit(solution)/shard_map/ppermute | solution.py:283
  65.3 0.0 collective-permute-start.3
  65.3 1.0 copy-done.1
  66.3 18.6 %project.7.refs_6_.refs_8_ = f32[64,512]{1,0:T(8,128)} custom-call(s32[1]{0:T(128)} %bitcast.shard_ref, bf16[2,512,512]{2,1,0:T(8,128)(2,1)} %split_blocks.2.refs_0_, bf16[2,512,512]{2,1,0:T(8,128)(2,1)} %collective-permute-done.refs_1_, bf16[7168,2048]{1,0:T(8,128)(2,1)} %refs_4_.11, bf16[7168,2048]{1,0:T(8,128)(2,1)} %collective-permute-done.2.refs_3_.refs_5_, ...), custom_call_target="tpu_custom_call" | custom-call | flops 10737418240 | bytes 26214400 | tf_op jit(solution)/shard_map/project/pallas_call | solution.py:149
  84.8 3.0 %collective-permute-done.7.refs_1_ = bf16[2,512,512]{2,1,0:T(8,128)(2,1)} collective-permute-done((bf16[2,512,512]{2,1,0:T(8,128)(2,1)}, bf16[2,512,512]{2,1,0:T(8,128)(2,1)}, u32[]{:S(2)}, u32[]{:S(2)}) %collective-permute-start.7) | collective-permute-done | bytes 1048608 | tf_op jit(solution)/shard_map/ppermute | solution.py:283
  87.8 0.0 collective-permute-start.10
  87.8 22.8 %project.8.refs_9_.refs_8_ = f32[7168,512]{1,0:T(8,128)} custom-call(s32[1]{0:T(128)} %bitcast.shard_ref, bf16[2,512,512]{2,1,0:T(8,128)(2,1)} %collective-permute-done.6.refs_0_, bf16[2,512,512]{2,1,0:T(8,128)(2,1)} %collective-permute-done.7.refs_1_, bf16[7168,2048]{1,0:T(8,128)(2,1)} %refs_4_.11, ...), custom_call_target="tpu_custom_call" | custom-call | flops 15032385536 | bytes 36700160 | tf_op jit(solution)/shard_map/project/pallas_call | solution.py:149
  110.7 13.1 %project.9.refs_8_ = f32[64,512]{1,0:T(8,128)} custom-call(s32[1]{0:T(128)} %bitcast.shard_ref, bf16[2,512,512]{2,1,0:T(8,128)(2,1)} %copy-done.1, bf16[2,512,512]{2,1,0:T(8,128)(2,1)} %collective-permute-done.3.refs_1_, bf16[7168,2048]{1,0:T(8,128)(2,1)} %refs_4_.11, bf16[7168,2048]{1,0:T(8,128)(2,1)} %collective-permute-done.2.refs_3_.refs_5_, ...), custom_call_target="tpu_custom_call" | custom-call | flops 6442450944 | bytes 15728640 | tf_op jit(solution)/shard_map/project/pallas_call | solution.py:149
  123.7 7.3 %collective-permute-done.10.refs_9_.refs_0_ = bf16[2,512,512]{2,1,0:T(8,128)(2,1)} collective-permute-done((bf16[2,512,512]{2,1,0:T(8,128)(2,1)}, bf16[2,512,512]{2,1,0:T(8,128)(2,1)}, u32[]{:S(2)}, u32[]{:S(2)}) %collective-permute-start.10) | collective-permute-done | bytes 1048608 | tf_op jit(solution)/shard_map/ppermute | solution.py:283
  131.0 0.0 collective-permute-start.15
  131.0 0.8 fusion
  131.8 1.6 collective-permute-start.17
  133.4 15.7 %project.10.refs_10_ = f32[64,512]{1,0:T(8,128)} custom-call(s32[1]{0:T(128)} %bitcast.shard_ref, bf16[2,512,512]{2,1,0:T(8,128)(2,1)} %copy-done.1, bf16[2,512,512]{2,1,0:T(8,128)(2,1)} %collective-permute-done.3.refs_1_, bf16[7168,2048]{1,0:T(8,128)(2,1)} %refs_4_.11, bf16[7168,2048]{1,0:T(8,128)(2,1)} %collective-permute-done.2.refs_3_.refs_5_, ...), custom_call_target="tpu_custom_call" | custom-call | flops 8589934592 | bytes 20971520 | tf_op jit(solution)/shard_map/project/pallas_call | solution.py:149
  149.1 0.9 pad_maximum_fusion.refs_0_
  150.0 1.6 collective-permute-done.11.refs_6_
  151.6 1.6 collective-permute-start.12
  153.2 1.3 collective-permute-start.13
  154.5 2.6 %collective-permute-start.14 = (f32[128,512]{1,0:T(8,128)S(1)}, f32[128,512]{1,0:T(8,128)}, u32[]{:S(2)}, u32[]{:S(2)}) collective-permute-start(f32[128,512]{1,0:T(8,128)S(1)} %pad_maximum_fusion.refs_0_), channel_id=1, source_target_pairs={{0,12},{1,13},{2,14},{3,15},{4,0},{5,1},{6,2},{7,3},{8,4},{9,5},{1... | collective-permute-start | bytes 786440 | tf_op jit(solution)/shard_map/ppermute | solution.py:300
  157.2 2.3 %collective-permute-done.15.refs_1_ = bf16[2,512,512]{2,1,0:T(8,128)(2,1)} collective-permute-done((bf16[2,512,512]{2,1,0:T(8,128)(2,1)}, bf16[2,512,512]{2,1,0:T(8,128)(2,1)}, u32[]{:S(2)}, u32[]{:S(2)}) %collective-permute-start.15) | collective-permute-done | bytes 1048608 | tf_op jit(solution)/shard_map/ppermute | solution.py:283
  159.4 1.5 collective-permute-start.16
  160.9 27.1 %project.11 = (f32[64,512]{1,0:T(8,128)}, f32[2048,512]{1,0:T(8,128)}) custom-call(s32[1]{0:T(128)} %bitcast.shard_ref, bf16[2,512,512]{2,1,0:T(8,128)(2,1)} %collective-permute-done.10.refs_9_.refs_0_, bf16[2,512,512]{2,1,0:T(8,128)(2,1)} %collective-permute-done.15.refs_1_, bf16[7168,2048]{1,0:T(8,128)(2,1)} %refs_4_.11, ...), custom_call_target="tpu_custom_call" | custom-call | flops 12884901888 | bytes 31457280 | tf_op jit(solution)/shard_map/project/pallas_call | solution.py:149
  188.0 4.9 %finish.2.before_ref = f32[64,512]{1,0:T(8,128)} custom-call(f32[2048,512]{1,0:T(8,128)} %get-tuple-element.43.hidden_ref, bf16[512,1536]{1,0:T(8,128)(2,1)} %collective-permute-done.17.gate_ref, bf16[64,7168]{1,0:T(8,128)(2,1)} %bitcast.9, f32[64,512]{1,0:T(8,128)} %get-tuple-element.46.before_ref), custom_call_target="tpu_custom_call" | custom-call | tf_op jit(solution)/shard_map/finish/pallas_call | solution.py:192
  193.0 1.3 collective-permute-done.16.gate_ref
  194.2 2.5 %finish.3 = bf16[64,512]{1,0:T(8,128)(2,1)} custom-call(f32[2048,512]{1,0:T(8,128)} %get-tuple-element.43.hidden_ref, bf16[512,512]{1,0:T(8,128)(2,1)} %collective-permute-done.16.gate_ref, bf16[64,7168]{1,0:T(8,128)(2,1)} %bitcast.10, f32[64,512]{1,0:T(8,128)} %finish.2.before_ref), custom_call_target="tpu_custom_call" | custom-call | tf_op jit(solution)/shard_map/finish/pallas_call | solution.py:192
  196.7 1.5 collective-permute-start.18
  198.2 1.6 collective-permute-start.19
  199.8 0.0 collective-permute-done.12.refs_1_
  199.8 2.3 %collective-permute-start.20 = (bf16[64,512]{1,0:T(8,128)(2,1)}, bf16[64,512]{1,0:T(8,128)(2,1)S(1)}, u32[]{:S(2)}, u32[]{:S(2)}) collective-permute-start(bf16[64,512]{1,0:T(8,128)(2,1)} %finish.3), channel_id=1, source_target_pairs={{0,10},{1,11},{2,8},{3,9},{4,14},{5,15},{6,12},{7,13},{8,2},{9,3},... | collective-permute-start | bytes 196616 | tf_op jit(solution)/shard_map/ppermute | solution.py:300
  202.1 0.0 collective-permute-done.13.refs_2_
  202.1 2.5 %collective-permute-start.21 = (bf16[64,512]{1,0:T(8,128)(2,1)}, bf16[64,512]{1,0:T(8,128)(2,1)S(1)}, u32[]{:S(2)}, u32[]{:S(2)}) collective-permute-start(bf16[64,512]{1,0:T(8,128)(2,1)} %finish.3), channel_id=1, source_target_pairs={{0,14},{1,15},{2,12},{3,13},{4,2},{5,3},{6,0},{7,1},{8,6},{9,7},{1... | collective-permute-start | bytes 196616 | tf_op jit(solution)/shard_map/ppermute | solution.py:300
  204.6 0.0 collective-permute-done.14.refs_3_
  204.6 0.0 collective-permute-done.18.refs_4_
  204.6 0.8 collective-permute-done.19.refs_5_
  205.4 0.7 collective-permute-done.20.refs_6_
  206.1 1.4 collective-permute-done.21.refs_7_
  207.5 0.6 copy-done.13
  208.1 3.6 %score.1 = f32[64,512]{1,0:T(8,128)} custom-call(f32[128,512]{1,0:T(8,128)} %copy-done.4, f32[128,512]{1,0:T(8,128)} %collective-permute-done.12.refs_1_, f32[128,512]{1,0:T(8,128)} %collective-permute-done.13.refs_2_, f32[128,512]{1,0:T(8,128)} %collective-permute-done.14.refs_3_, bf16[64,512]{1,0:T(8,128)(2,1)} %copy-done.10, bf16[64,512]{1,0:T(8,128)(2,1)} %copy-done.11, ...), custom_call_target="tpu_custom_call" | custom-call | tf_op jit(solution)/shard_map/score/pallas_call | solution.py:255
  (26 shorter events, 0.1 us)
Async XLA Ops:
  0.0 131.0 %copy-start = (bf16[512,2048]{1,0:T(8,128)(2,1)S(1)}, bf16[512,2048]{1,0:T(8,128)(2,1)}, u32[]{:S(2)}) copy-start(bf16[512,2048]{1,0:T(8,128)(2,1)} %param.7) | copy-start | bytes 6291460
  0.0 11.4 %copy-start.6 = (bf16[64,1024]{1,0:T(8,128)(2,1)S(1)}, bf16[64,1024]{1,0:T(8,128)(2,1)}, u32[]{:S(2)}) copy-start(bf16[64,1024]{1,0:T(8,128)(2,1)} %refs_0_) | copy-start | bytes 393220
  0.0 43.6 %collective-permute-start.2 = (bf16[7168,2048]{1,0:T(8,128)(2,1)}, bf16[7168,2048]{1,0:T(8,128)(2,1)}, u32[]{:S(2)}, u32[]{:S(2)}) collective-permute-start(bf16[7168,2048]{1,0:T(8,128)(2,1)} %refs_4_.11), channel_id=1, source_target_pairs={{0,1},{1,0},{2,3},{3,2},{4,5},{5,4},{6,7},{7,6},{8,9},{9,8},{10,11... | collective-permute-start | bytes 88080392 | tf_op jit(solution)/shard_map/ppermute | solution.py:18
  1.8 2.8 %copy-start.2 = (bf16[512,1024]{1,0:T(8,128)(2,1)}, bf16[512,1024]{1,0:T(8,128)(2,1)S(1)}, u32[]{:S(2)}) copy-start(bf16[512,1024]{1,0:T(8,128)(2,1)S(1)} %slice.12.refs_0_) | copy-start | bytes 3145732
  1.8 29.2 %collective-permute-start.4 = (bf16[512,1024]{1,0:T(8,128)(2,1)S(1)}, bf16[512,1024]{1,0:T(8,128)(2,1)}, u32[]{:S(2)}, u32[]{:S(2)}) collective-permute-start(bf16[512,1024]{1,0:T(8,128)(2,1)S(1)} %slice.12.refs_0_), channel_id=1, source_target_pairs={{0,2},{1,3},{2,0},{3,1},{4,6},{5,7},{6,4},{7,5},{8,10},{9,11},{10,... | collective-permute-start | bytes 3145736 | tf_op jit(solution)/shard_map/ppermute | solution.py:18
  9.9 27.3 %collective-permute-start = (bf16[2,512,512]{2,1,0:T(8,128)(2,1)}, bf16[2,512,512]{2,1,0:T(8,128)(2,1)}, u32[]{:S(2)}, u32[]{:S(2)}) collective-permute-start(bf16[2,512,512]{2,1,0:T(8,128)(2,1)} %split_blocks.2.refs_0_), channel_id=1, source_target_pairs={{0,4},{4,8},{8,12},{12,0},{1,5},{5,9},{9,13},{13,1},{2,6},{6,10},{... | collective-permute-start | bytes 3145736 | tf_op jit(solution)/shard_map/ppermute | solution.py:283
  11.4 19.5 %collective-permute-start.5 = (bf16[64,1024]{1,0:T(8,128)(2,1)S(1)}, bf16[64,1024]{1,0:T(8,128)(2,1)S(1)}, u32[]{:S(2)}, u32[]{:S(2)}) collective-permute-start(bf16[64,1024]{1,0:T(8,128)(2,1)S(1)} %copy-done.6), channel_id=1, source_target_pairs={{0,2},{1,3},{2,0},{3,1},{4,6},{5,7},{6,4},{7,5},{8,10},{9,11},{10,... | collective-permute-start | bytes 393224 | tf_op jit(solution)/shard_map/ppermute | solution.py:18
  31.0 22.7 %copy-start.7 = (bf16[64,1024]{1,0:T(8,128)(2,1)}, bf16[64,1024]{1,0:T(8,128)(2,1)S(1)}, u32[]{:S(2)}) copy-start(bf16[64,1024]{1,0:T(8,128)(2,1)S(1)} %collective-permute-done.5.refs_1_) | copy-start | bytes 393220
  31.0 25.3 %collective-permute-start.6 = (bf16[2,512,512]{2,1,0:T(8,128)(2,1)}, bf16[2,512,512]{2,1,0:T(8,128)(2,1)}, u32[]{:S(2)}, u32[]{:S(2)}) collective-permute-start(bf16[2,512,512]{2,1,0:T(8,128)(2,1)} %split_blocks.3), channel_id=1, source_target_pairs={{0,2},{1,3},{2,0},{3,1},{4,6},{5,7},{6,4},{7,5},{8,10},{9,11},{10,... | collective-permute-start | bytes 3145736 | tf_op jit(solution)/shard_map/ppermute | solution.py:18
  37.1 28.1 %collective-permute-start.1 = (bf16[2,512,512]{2,1,0:T(8,128)(2,1)}, bf16[2,512,512]{2,1,0:T(8,128)(2,1)S(1)}, u32[]{:S(2)}, u32[]{:S(2)}) collective-permute-start(bf16[2,512,512]{2,1,0:T(8,128)(2,1)} %collective-permute-done.refs_1_), channel_id=1, source_target_pairs={{0,4},{4,8},{8,12},{12,0},{1,5},{5,9},{9,13},{13,1},{2,6},{6,10},{... | collective-permute-start | bytes 3145736 | tf_op jit(solution)/shard_map/ppermute | solution.py:283
  37.2 22.2 %collective-permute-start.8 = (bf16[64,1024]{1,0:T(8,128)(2,1)S(1)}, bf16[64,1024]{1,0:T(8,128)(2,1)S(1)}, u32[]{:S(2)}, u32[]{:S(2)}) collective-permute-start(bf16[64,1024]{1,0:T(8,128)(2,1)S(1)} %copy-done.6), channel_id=1, source_target_pairs={{0,1},{1,0},{2,3},{3,2},{4,5},{5,4},{6,7},{7,6},{8,9},{9,8},{10,11... | collective-permute-start | bytes 393224 | tf_op jit(solution)/shard_map/ppermute | solution.py:18
  37.2 22.2 %collective-permute-start.9 = (bf16[64,1024]{1,0:T(8,128)(2,1)S(1)}, bf16[64,1024]{1,0:T(8,128)(2,1)S(1)}, u32[]{:S(2)}, u32[]{:S(2)}) collective-permute-start(bf16[64,1024]{1,0:T(8,128)(2,1)S(1)} %collective-permute-done.5.refs_1_), channel_id=1, source_target_pairs={{0,1},{1,0},{2,3},{3,2},{4,5},{5,4},{6,7},{7,6},{8,9},{9,8},{10,11... | collective-permute-start | bytes 393224 | tf_op jit(solution)/shard_map/ppermute | solution.py:18
  56.3 31.5 %collective-permute-start.7 = (bf16[2,512,512]{2,1,0:T(8,128)(2,1)}, bf16[2,512,512]{2,1,0:T(8,128)(2,1)}, u32[]{:S(2)}, u32[]{:S(2)}) collective-permute-start(bf16[2,512,512]{2,1,0:T(8,128)(2,1)} %collective-permute-done.6.refs_0_), channel_id=1, source_target_pairs={{0,4},{4,8},{8,12},{12,0},{1,5},{5,9},{9,13},{13,1},{2,6},{6,10},{... | collective-permute-start | bytes 3145736 | tf_op jit(solution)/shard_map/ppermute | solution.py:283
  57.8 93.8 %collective-permute-start.11 = (bf16[512,4096]{1,0:T(8,128)(2,1)}, bf16[512,4096]{1,0:T(8,128)(2,1)}, u32[]{:S(2)}, u32[]{:S(2)}) collective-permute-start(bf16[512,4096]{1,0:T(8,128)(2,1)} %slice.13), channel_id=1, source_target_pairs={{0,2},{1,3},{2,0},{3,1},{4,6},{5,7},{6,4},{7,5},{8,10},{9,11},{10,... | collective-permute-start | bytes 12582920 | tf_op jit(solution)/shard_map/ppermute | solution.py:18
  59.3 0.7 copy-start.8
  60.0 0.7 copy-start.9
  65.3 1.0 copy-start.1
  65.3 45.4 %collective-permute-start.3 = (bf16[2,512,512]{2,1,0:T(8,128)(2,1)S(1)}, bf16[2,512,512]{2,1,0:T(8,128)(2,1)}, u32[]{:S(2)}, u32[]{:S(2)}) collective-permute-start(bf16[2,512,512]{2,1,0:T(8,128)(2,1)S(1)} %collective-permute-done.1.refs_9_.refs_0_), channel_id=1, source_target_pairs={{0,4},{4,8},{8,12},{12,0},{1,5},{5,9},{9,13},{13,1},{2,6},{6,10},{... | collective-permute-start | bytes 3145736 | tf_op jit(solution)/shard_map/ppermute | solution.py:283
  87.8 43.2 %collective-permute-start.10 = (bf16[2,512,512]{2,1,0:T(8,128)(2,1)}, bf16[2,512,512]{2,1,0:T(8,128)(2,1)}, u32[]{:S(2)}, u32[]{:S(2)}) collective-permute-start(bf16[2,512,512]{2,1,0:T(8,128)(2,1)} %collective-permute-done.7.refs_1_), channel_id=1, source_target_pairs={{0,4},{4,8},{8,12},{12,0},{1,5},{5,9},{9,13},{13,1},{2,6},{6,10},{... | collective-permute-start | bytes 3145736 | tf_op jit(solution)/shard_map/ppermute | solution.py:283
  110.7 20.4 %copy-start.5 = (bf16[2048,64]{0,1:T(8,128)(2,1)S(1)}, bf16[2048,64]{0,1:T(8,128)(2,1)}, u32[]{:S(2)}) copy-start(bf16[2048,64]{0,1:T(8,128)(2,1)} %param.11) | copy-start | bytes 786436
  110.7 21.1 %copy-start.3 = (bf16[512,1536]{1,0:T(8,128)(2,1)S(1)}, bf16[512,1536]{1,0:T(8,128)(2,1)}, u32[]{:S(2)}) copy-start(bf16[512,1536]{1,0:T(8,128)(2,1)} %slice.14) | copy-start | bytes 4718596
  131.0 28.4 %collective-permute-start.15 = (bf16[2,512,512]{2,1,0:T(8,128)(2,1)}, bf16[2,512,512]{2,1,0:T(8,128)(2,1)}, u32[]{:S(2)}, u32[]{:S(2)}) collective-permute-start(bf16[2,512,512]{2,1,0:T(8,128)(2,1)} %collective-permute-done.10.refs_9_.refs_0_), channel_id=1, source_target_pairs={{0,4},{4,8},{8,12},{12,0},{1,5},{5,9},{9,13},{13,1},{2,6},{6,10},{... | collective-permute-start | bytes 3145736 | tf_op jit(solution)/shard_map/ppermute | solution.py:283
  131.8 56.2 %collective-permute-start.17 = (bf16[512,1536]{1,0:T(8,128)(2,1)S(1)}, bf16[512,1536]{1,0:T(8,128)(2,1)}, u32[]{:S(2)}, u32[]{:S(2)}) collective-permute-start(bf16[512,1536]{1,0:T(8,128)(2,1)S(1)} %copy-done.3), channel_id=1, source_target_pairs={{0,2},{1,3},{2,0},{3,1},{4,6},{5,7},{6,4},{7,5},{8,10},{9,11},{10,... | collective-permute-start | bytes 4718600 | tf_op jit(solution)/shard_map/ppermute | solution.py:18
  150.0 38.0 %copy-start.4 = (f32[128,512]{1,0:T(8,128)}, f32[128,512]{1,0:T(8,128)S(1)}, u32[]{:S(2)}) copy-start(f32[128,512]{1,0:T(8,128)S(1)} %pad_maximum_fusion.refs_0_) | copy-start | bytes 786436
  151.6 48.2 %collective-permute-start.12 = (f32[128,512]{1,0:T(8,128)S(1)}, f32[128,512]{1,0:T(8,128)}, u32[]{:S(2)}, u32[]{:S(2)}) collective-permute-start(f32[128,512]{1,0:T(8,128)S(1)} %pad_maximum_fusion.refs_0_), channel_id=1, source_target_pairs={{0,4},{1,5},{2,6},{3,7},{4,8},{5,9},{6,10},{7,11},{8,12},{9,13},{1... | collective-permute-start | bytes 786440 | tf_op jit(solution)/shard_map/ppermute | solution.py:300
  153.2 48.9 %collective-permute-start.13 = (f32[128,512]{1,0:T(8,128)S(1)}, f32[128,512]{1,0:T(8,128)}, u32[]{:S(2)}, u32[]{:S(2)}) collective-permute-start(f32[128,512]{1,0:T(8,128)S(1)} %pad_maximum_fusion.refs_0_), channel_id=1, source_target_pairs={{0,8},{1,9},{2,10},{3,11},{4,12},{5,13},{6,14},{7,15},{8,0},{9,1},... | collective-permute-start | bytes 786440 | tf_op jit(solution)/shard_map/ppermute | solution.py:300
  154.5 50.1 %collective-permute-start.14 = (f32[128,512]{1,0:T(8,128)S(1)}, f32[128,512]{1,0:T(8,128)}, u32[]{:S(2)}, u32[]{:S(2)}) collective-permute-start(f32[128,512]{1,0:T(8,128)S(1)} %pad_maximum_fusion.refs_0_), channel_id=1, source_target_pairs={{0,12},{1,13},{2,14},{3,15},{4,0},{5,1},{6,2},{7,3},{8,4},{9,5},{1... | collective-permute-start | bytes 786440 | tf_op jit(solution)/shard_map/ppermute | solution.py:300
  159.4 34.8 %collective-permute-start.16 = (bf16[512,512]{1,0:T(8,128)(2,1)}, bf16[512,512]{1,0:T(8,128)(2,1)}, u32[]{:S(2)}, u32[]{:S(2)}) collective-permute-start(bf16[512,512]{1,0:T(8,128)(2,1)} %slice.15), channel_id=1, source_target_pairs={{0,2},{1,3},{2,0},{3,1},{4,6},{5,7},{6,4},{7,5},{8,10},{9,11},{10,... | collective-permute-start | bytes 1572872 | tf_op jit(solution)/shard_map/ppermute | solution.py:18
  196.7 7.9 %collective-permute-start.18 = (bf16[64,512]{1,0:T(8,128)(2,1)}, bf16[64,512]{1,0:T(8,128)(2,1)S(1)}, u32[]{:S(2)}, u32[]{:S(2)}) collective-permute-start(bf16[64,512]{1,0:T(8,128)(2,1)} %finish.3), channel_id=1, source_target_pairs={{0,2},{1,3},{2,0},{3,1},{4,6},{5,7},{6,4},{7,5},{8,10},{9,11},{10,... | collective-permute-start | bytes 196616 | tf_op jit(solution)/shard_map/ppermute | solution.py:300
  198.2 7.2 %collective-permute-start.19 = (bf16[64,512]{1,0:T(8,128)(2,1)}, bf16[64,512]{1,0:T(8,128)(2,1)S(1)}, u32[]{:S(2)}, u32[]{:S(2)}) collective-permute-start(bf16[64,512]{1,0:T(8,128)(2,1)} %finish.3), channel_id=1, source_target_pairs={{0,6},{1,7},{2,4},{3,5},{4,10},{5,11},{6,8},{7,9},{8,14},{9,15},{1... | collective-permute-start | bytes 196616 | tf_op jit(solution)/shard_map/ppermute | solution.py:300
  199.8 6.3 %collective-permute-start.20 = (bf16[64,512]{1,0:T(8,128)(2,1)}, bf16[64,512]{1,0:T(8,128)(2,1)S(1)}, u32[]{:S(2)}, u32[]{:S(2)}) collective-permute-start(bf16[64,512]{1,0:T(8,128)(2,1)} %finish.3), channel_id=1, source_target_pairs={{0,10},{1,11},{2,8},{3,9},{4,14},{5,15},{6,12},{7,13},{8,2},{9,3},... | collective-permute-start | bytes 196616 | tf_op jit(solution)/shard_map/ppermute | solution.py:300
  202.1 5.4 %collective-permute-start.21 = (bf16[64,512]{1,0:T(8,128)(2,1)}, bf16[64,512]{1,0:T(8,128)(2,1)S(1)}, u32[]{:S(2)}, u32[]{:S(2)}) collective-permute-start(bf16[64,512]{1,0:T(8,128)(2,1)} %finish.3), channel_id=1, source_target_pairs={{0,14},{1,15},{2,12},{3,13},{4,2},{5,3},{6,0},{7,1},{8,6},{9,7},{1... | collective-permute-start | bytes 196616 | tf_op jit(solution)/shard_map/ppermute | solution.py:300
  204.6 2.8 %copy-start.10 = (bf16[64,512]{1,0:T(8,128)(2,1)}, bf16[64,512]{1,0:T(8,128)(2,1)S(1)}, u32[]{:S(2)}) copy-start(bf16[64,512]{1,0:T(8,128)(2,1)S(1)} %collective-permute-done.18.refs_4_) | copy-start | bytes 196612
  205.4 2.1 copy-start.11
  206.1 1.4 copy-start.12
  207.5 0.6 copy-start.13
